TPU v7x, 512 devices: a whole 4x8x8 slice. The times are simulated.
512 devices in a mesh: gx: 16 (over x_lo, z), gy: 32 (over y, x_hi, core).
Axes of the slice: x: 4 (x_hi: 2, x_lo: 2; x = x_hi * 2 + x_lo), y: 8, z: 8, core: 2. Of those that a mesh axis runs over, the one named last changes fastest.
Arguments:
- features_in: bfloat16 [16, 32, 12, 128, 128], P('gx', 'gy'), may hold values from -6 to 6
- pre_act: bfloat16 [16, 32, 12, 128, 128], P('gx', 'gy'), may hold values from -6 to 6
- cotangent: bfloat16 [16, 32, 12, 128, 128], P('gx', 'gy'), may hold values from -6 to 6
- w_first: bfloat16 [27, 128, 128], replicated, may hold values from -0.375 to 0.375
- w_second: bfloat16 [27, 128, 128], replicated, may hold values from -0.375 to 0.375
- in_slots: int32 [16, 32, 27, 7], P('gx', 'gy'), may hold values from 0 to 28, as said below
- out_slots: int32 [16, 32, 27, 7], P('gx', 'gy'), may hold values from 0 to 12, as said below
- send_lists: int32 [16, 32, 8, 2], P('gx', 'gy'), may hold values from 0 to 11, as said below
Outputs:
- input_grad: bfloat16 [16, 32, 12, 128, 128], P('gx', 'gy')
- weight_grads: float32 [6912, 128], P('gy', 'gx')
Inputs may be any that keep to these rules, and one draw needn't show every extreme that they name: `in_slots`: for each device and offset the used entries come first and are distinct slots of the extended blocks; the remaining entries equal 28, the zero block. Every device has some offset with all 7 entries used. `out_slots`: an entry is used exactly where the same entry of in_slots is; used entries of one offset are distinct local blocks, unused ones equal 12. `send_lists`: every device lists exactly 2 distinct local blocks for each heading, also at the grid's edge where nobody receives them.
All inputs are finite; a program needn't handle non-finite values.
Results may differ from a plain program's by a relative error of at most 0.0058.
Values may be sent and summed in bfloat16 or wider, within the bound.
A program may use at most 128 MiB of HBM per device.

v0:
```python
import math

import jax
import jax.numpy as jnp
from jax import lax
from jax.sharding import PartitionSpec as P

HEADINGS = ((-1, -1), (-1, 0), (-1, 1), (0, -1), (0, 1), (1, -1), (1, 0), (1, 1))


def shifted(value, axis, steps):
    count = lax.axis_size(axis)
    leading, last = (max(0, -steps), min(count, count - steps))
    return lax.ppermute(value, axis, [(source, source + steps) for source in range(leading, last)])


def parcel_east_west(parcel, stride, cargo):
    if cargo == "features":
        return shifted(parcel, "gx", stride)
    return shifted(parcel, "gx", stride)


def parcel_north_south(parcel, stride, cargo):
    if cargo == "features":
        return shifted(parcel, "gy", stride)
    return shifted(parcel, "gy", stride)


def travel(parcels, cargo):
    arrived = []
    for heading in range(8):
        step_x, step_y = HEADINGS[heading]
        parcel = parcels[heading]
        if step_x != 0:
            parcel = parcel_east_west(parcel, step_x, cargo)
        if step_y != 0:
            parcel = parcel_north_south(parcel, step_y, cargo)
        arrived.append(parcel)
    return jnp.stack(arrived)


def one_hot(indices, extent, dtype):
    return (indices[:, None] == lax.iota(jnp.int32, extent)[None, :]).astype(dtype)


def offsets_back(source_ext, grad_ext, weight, slot_in, slot_out):
    channels = source_ext.shape[-1]
    ext_rows = source_ext.shape[0]

    def per_offset(carry, inputs):
        offset_weight, in_row, out_row = inputs
        sources = jnp.take(source_ext, in_row, axis=0).reshape(-1, channels)
        grad_rows = jnp.take(grad_ext, out_row, axis=0).reshape(-1, channels)
        weight_grad = lax.dot_general(
            sources, grad_rows, (((0,), (0,)), ((), ())), preferred_element_type=jnp.float32
        )
        back_rows = lax.dot_general(
            grad_rows, offset_weight, (((1,), (1,)), ((), ())), preferred_element_type=jnp.float32
        )
        return (carry, (weight_grad, back_rows.reshape(in_row.shape[0], -1)))

    start = jnp.zeros((), jnp.float32)
    _, (weight_grads, back_all) = lax.scan(per_offset, start, (weight, slot_in, slot_out))
    back_all = back_all.reshape(-1, back_all.shape[-1])
    running = jax.ops.segment_sum(back_all, slot_in.reshape(-1), num_segments=ext_rows)
    return (running.reshape(source_ext.shape), weight_grads)


def give_back(partial_value, blocks, send_rows):
    halo_rows = send_rows.shape[0] * send_rows.shape[1]
    halo_part = partial_value[blocks : blocks + halo_rows].astype(jnp.bfloat16)
    halo_part = halo_part.reshape(send_rows.shape + partial_value.shape[1:])
    returned = travel(halo_part[::-1], "grads")[::-1]
    returned = returned.reshape(halo_rows, -1).astype(jnp.float32)
    pick_back = one_hot(send_rows.reshape(-1), blocks, jnp.float32)
    placed = lax.dot_general(
        pick_back,
        returned,
        (((0,), (0,)), ((), ())),
        precision=lax.Precision.HIGHEST,
        preferred_element_type=jnp.float32,
    )
    return partial_value[:blocks] + placed.reshape((blocks,) + partial_value.shape[1:])


def per_device(features_in, pre_act, cotangent, w_first, w_second, in_slots, out_slots, send_lists):
    own_feat = features_in[0, 0]
    own_pre = pre_act[0, 0]
    own_grad = cotangent[0, 0]
    slot_map_in = in_slots[0, 0]
    slot_map_out = out_slots[0, 0]
    send_rows = send_lists[0, 0]
    blocks = own_feat.shape[0]
    halo_rows = send_rows.shape[0] * send_rows.shape[1]
    block_shape = own_feat.shape[1:]
    padding = jnp.zeros((1,) + block_shape, jnp.bfloat16)
    flat_send = send_rows.reshape(-1)
    chosen_feat = jnp.take(own_feat, flat_send, axis=0)
    chosen_pre = jnp.take(own_pre, flat_send, axis=0)
    chosen_feat = chosen_feat.reshape(send_rows.shape + block_shape)
    chosen_pre = chosen_pre.reshape(send_rows.shape + block_shape)
    parcels = jnp.stack([chosen_feat, chosen_pre], axis=1)
    arrived = travel(parcels, "features")
    halo_feat = arrived[:, 0].reshape((halo_rows,) + block_shape)
    halo_pre = arrived[:, 1].reshape((halo_rows,) + block_shape)
    pre_ext = jnp.concatenate([own_pre, halo_pre, padding], axis=0)
    act_ext = jax.nn.silu(pre_ext.astype(jnp.float32)).astype(jnp.bfloat16)
    grad_ext = jnp.concatenate([own_grad, padding], axis=0)
    second_part, second_weight = offsets_back(
        act_ext, grad_ext, w_second, slot_map_in, slot_map_out
    )
    act_grad = give_back(second_part, blocks, send_rows)
    pre_value = own_pre.astype(jnp.float32)
    sigmoid_value = jax.nn.sigmoid(pre_value)
    silu_slope = sigmoid_value * (1.0 + pre_value * (1.0 - sigmoid_value))
    pre_grad = (act_grad * silu_slope).astype(jnp.bfloat16)
    feat_ext = jnp.concatenate([own_feat, halo_feat, padding], axis=0)
    pre_grad_ext = jnp.concatenate([pre_grad, padding], axis=0)
    first_part, first_weight = offsets_back(
        feat_ext, pre_grad_ext, w_first, slot_map_in, slot_map_out
    )
    input_grad = give_back(first_part, blocks, send_rows).astype(jnp.bfloat16)
    weight_term = jnp.concatenate([first_weight, second_weight], axis=0).reshape(
        -1, own_feat.shape[-1]
    )
    grad_norm = slot_map_in.shape[-1] * block_shape[0] * lax.axis_size("gx") * lax.axis_size("gy")
    reduced = lax.psum_scatter(weight_term, "gy", scatter_dimension=0, tiled=True)
    reduced = lax.psum_scatter(reduced, "gx", scatter_dimension=1, tiled=True)
    weight_grads = reduced * (1.0 / math.sqrt(grad_norm))
    return (input_grad[None, None], weight_grads)


def solution(mesh):
    in_specs = (
        P("gx", "gy", None, None, None),
        P("gx", "gy", None, None, None),
        P("gx", "gy", None, None, None),
        P(),
        P(),
        P("gx", "gy", None, None),
        P("gx", "gy", None, None),
        P("gx", "gy", None, None),
    )
    out_specs = (P("gx", "gy", None, None, None), P("gy", "gx"))
    return jax.shard_map(
        per_device, mesh=mesh, in_specs=in_specs, out_specs=out_specs, check_vma=False
    )
```

profile of v0, /device:TPU:24, one launch (start us, length us, event | category | flops | bytes accessed | tf_op | source)
XLA Modules:
  0.0 664.7 jit_solution(1379848483761269768)
XLA Ops:
  13.0 6.5 collective-permute-done
  19.5 3.7 collective-permute-start.1
  25.8 3.1 collective-permute-start.5
  28.9 1.9 collective-permute-start.6
  31.3 5.7 collective-permute-start.7
  37.0 4.3 collective-permute-start.10
  41.3 2.1 collective-permute-start.4
  43.4 5.5 collective-permute-start.9
  48.9 5.6 collective-permute-start.8
  54.5 1.9 collective-permute-start.11
  57.1 6.3 collective-permute-done.11
  65.8 6.6 broadcast.59.clone
  72.7 130.6 %while.24 = (s32[]{:T(128)}, f32[27,128,128]{2,1,0:T(8,128)S(1)}, f32[27,7,16384]{2,1,0:T(8,128)}, s32[27,7]{1,0:T(8,128)S(1)}, bf16[29,128,128]{2,1,0:T(8,128)(...) while((s32[]{:T(128)}, f32[27,128,128]{2,1,0:T(8,128)S(1)}, ...), condition=%wide.region_1.5_spmd, body=%wide.region_0.4_spmd.sunk | while | flops 58951764 | bytes 4532058 | solution.py:63
  73.4 1.8 gather_fusion.1
  78.2 1.8 gather_fusion.1
  92.8 1.8 gather_fusion.1
  107.3 1.8 gather_fusion.1
  116.9 1.8 gather_fusion.1
  126.6 1.8 gather_fusion.1
  141.1 1.8 gather_fusion.1
  165.3 1.8 gather_fusion.1
  189.5 1.8 gather_fusion.1
  199.2 1.8 gather_fusion.1
  204.4 10.6 %reshape.152 = f32[189,16384]{1,0:T(8,128)} reshape(f32[27,7,16384]{2,1,0:T(8,128)} %get-tuple-element.91) | data formatting | bytes 24772608 | tf_op jit(solution)/shard_map/reshape | solution.py:64
  215.0 19.6 %scatter_custom_fusion = f32[29,16384]{1,0:T(8,128)S(1)} fusion(s32[189]{0:T(256)S(1)} %reshape.158, f32[189,16384]{1,0:T(8,128)} %reshape.152, f32[]{:T(128)} %constant.50.clone.1), kind=kCustom, calls=%fused_computation.88 | custom fusion | flops 3096576 | bytes 1901056 | tf_op jit(solution)/shard_map/scatter-add | solution.py:65
  239.1 3.1 collective-permute-done.12
  242.2 1.9 collective-permute-start.13
  245.4 3.8 collective-permute-start.17
  249.2 1.9 collective-permute-start.18
  251.5 3.7 collective-permute-start.19
  255.3 3.9 collective-permute-start.22
  259.2 3.1 collective-permute-start.16
  262.3 4.1 collective-permute-start.21
  266.4 4.5 collective-permute-start.20
  270.9 1.9 collective-permute-start.23
  273.0 5.9 collective-permute-done.23
  280.3 6.6 broadcast.59
  288.4 147.3 %while.25 = (s32[]{:T(128)}, f32[27,128,128]{2,1,0:T(8,128)}, f32[27,7,16384]{2,1,0:T(8,128)}, s32[27,7]{1,0:T(8,128)S(1)}, bf16[29,128,128]{2,1,0:T(8,128)(2,1)...) while((s32[]{:T(128)}, f32[27,128,128]{2,1,0:T(8,128)}, ...), condition=%wide.region_4.8_spmd, body=%wide.region_3.7_spmd.sunk | while | flops 58951764 | bytes 4532061 | solution.py:63
  305.5 1.8 gather_fusion.3
  327.3 1.8 gather_fusion.3
  343.6 1.8 gather_fusion.3
  354.6 1.8 gather_fusion.3
  360.0 1.8 gather_fusion.3
  365.4 1.8 gather_fusion.3
  370.9 1.8 gather_fusion.3
  387.3 1.8 gather_fusion.3
  420.0 1.8 gather_fusion.3
  425.5 1.8 gather_fusion.3
  430.9 1.8 gather_fusion.3
  435.6 3.6 pad_maximum_fusion
  439.4 10.6 %reshape.160 = f32[189,16384]{1,0:T(8,128)} reshape(f32[27,7,16384]{2,1,0:T(8,128)} %get-tuple-element.92) | data formatting | bytes 24772608 | tf_op jit(solution)/shard_map/reshape | solution.py:64
  450.0 18.7 %scatter_custom_fusion.1 = f32[29,16384]{1,0:T(8,128)S(1)} fusion(s32[189]{0:T(256)S(1)} %reshape.158, f32[189,16384]{1,0:T(8,128)} %reshape.160, f32[]{:T(128)} %constant.50.clone.1), kind=kCustom, calls=%fused_computation.86 | custom fusion | flops 3096576 | bytes 1901056 | tf_op jit(solution)/shard_map/scatter-add | solution.py:65
  470.6 4.9 collective-permute-done.24
  475.4 1.9 collective-permute-start.25
  480.1 2.9 collective-permute-start.29
  483.0 1.9 collective-permute-start.30
  485.3 5.2 collective-permute-start.31
  490.5 3.6 collective-permute-start.34
  494.2 5.2 collective-permute-start.28
  499.4 4.1 collective-permute-start.33
  503.5 3.8 collective-permute-start.32
  507.3 1.9 collective-permute-start.35
  509.4 71.3 %reduce-scatter.9.cloned.1.call-done = f32[216,128]{1,0:T(8,128)} async-done(((f32[6912,128]{1,0:T(8,128)}), f32[216,128]{1,0:T(8,128)}) %reduce-scatter.9.cloned.1.call-update) | async-done | bytes 110608
  584.1 72.0 %reduce-scatter.7.cloned.1.call-done = f32[8,216]{1,0:T(8,128)} async-done(((f32[128,216]{1,0:T(8,128)}), f32[8,216]{1,0:T(8,128)}) %reduce-scatter.7.cloned.1.call-update) | async-done | bytes 6928
  (661 shorter events, 269.0 us)
Async XLA Ops:
  7.2 573.5 %reduce-scatter.9.cloned.1.call-start = ((), (), s32[]{:S(2)}) async-start(), calls=%async_computation.3 | async-start | bytes 3649536
  11.4 19.4 %copy-start.7 = (s32[1,1,27,7]{2,1,3,0:T(1,128)S(1)}, s32[1,1,27,7]{2,1,3,0:T(1,128)}, u32[]{:S(2)}) copy-start(s32[1,1,27,7]{2,1,3,0:T(1,128)} %param.23) | copy-start | bytes 2272
  11.4 19.5 %copy-start.8 = (s32[1,1,27,7]{2,1,3,0:T(1,128)S(1)}, s32[1,1,27,7]{2,1,3,0:T(1,128)}, u32[]{:S(2)}) copy-start(s32[1,1,27,7]{2,1,3,0:T(1,128)} %param.24) | copy-start | bytes 2272
  11.4 19.7 %copy-start.6 = (bf16[1,1,12,128,128]{4,3,2,1,0:T(8,128)(2,1)S(1)}, bf16[1,1,12,128,128]{4,3,2,1,0:T(8,128)(2,1)}, u32[]{:S(2)}) copy-start(bf16[1,1,12,128,128]{4,3,2,1,0:T(8,128)(2,1)} %param.20) | copy-start | bytes 1179652
  11.7 7.8 %collective-permute-start = (bf16[2,2,128,128]{3,2,1,0:T(8,128)(2,1)S(1)}, bf16[2,2,128,128]{3,2,1,0:T(8,128)(2,1)S(1)}, u32[]{:S(2)}, u32[]{:S(2)}) collective-permute-start(bf16[2,2,128,128]{3,2,1,0:T(8,128)(2,1)S(1)} %get-tuple-element.188), channel_id=1, source_target_pairs={{32,0},{64,32},{96,64},{128,96},{160,128},{192,160},{224,192},{256... | collective-permute-start | bytes 393224 | tf_op jit(solution)/shard_map/ppermute | solution.py:14
  19.5 11.8 %collective-permute-start.1 = (bf16[2,2,128,128]{3,2,1,0:T(8,128)(2,1)S(1)}, bf16[2,2,128,128]{3,2,1,0:T(8,128)(2,1)S(1)}, u32[]{:S(2)}, u32[]{:S(2)}) collective-permute-start(bf16[2,2,128,128]{3,2,1,0:T(8,128)(2,1)S(1)} %collective-permute-done), channel_id=1, source_target_pairs={{1,0},{2,1},{3,2},{4,3},{5,4},{6,5},{7,6},{8,7},{9,8},{10,9},{11,1... | collective-permute-start | bytes 393224 | tf_op jit(solution)/shard_map/ppermute | solution.py:14
  23.2 13.8 %collective-permute-start.2 = (bf16[2,2,128,128]{3,2,1,0:T(8,128)(2,1)S(1)}, bf16[2,2,128,128]{3,2,1,0:T(8,128)(2,1)S(1)}, u32[]{:S(2)}, u32[]{:S(2)}) collective-permute-start(bf16[2,2,128,128]{3,2,1,0:T(8,128)(2,1)S(1)} %get-tuple-element.189), channel_id=1, source_target_pairs={{32,0},{64,32},{96,64},{128,96},{160,128},{192,160},{224,192},{256... | collective-permute-start | bytes 393224 | tf_op jit(solution)/shard_map/ppermute | solution.py:14
  24.5 16.8 %collective-permute-start.3 = (bf16[2,2,128,128]{3,2,1,0:T(8,128)(2,1)S(1)}, bf16[2,2,128,128]{3,2,1,0:T(8,128)(2,1)S(1)}, u32[]{:S(2)}, u32[]{:S(2)}) collective-permute-start(bf16[2,2,128,128]{3,2,1,0:T(8,128)(2,1)S(1)} %get-tuple-element.190), channel_id=1, source_target_pairs={{32,0},{64,32},{96,64},{128,96},{160,128},{192,160},{224,192},{256... | collective-permute-start | bytes 393224 | tf_op jit(solution)/shard_map/ppermute | solution.py:14
  25.8 30.7 %collective-permute-start.5 = (bf16[2,2,128,128]{3,2,1,0:T(8,128)(2,1)S(1)}, bf16[2,2,128,128]{3,2,1,0:T(8,128)(2,1)S(1)}, u32[]{:S(2)}, u32[]{:S(2)}) collective-permute-start(bf16[2,2,128,128]{3,2,1,0:T(8,128)(2,1)S(1)} %get-tuple-element.191), channel_id=1, source_target_pairs={{1,0},{2,1},{3,2},{4,3},{5,4},{6,5},{7,6},{8,7},{9,8},{10,9},{11,1... | collective-permute-start | bytes 393224 | tf_op jit(solution)/shard_map/ppermute | solution.py:14
  28.9 27.6 %collective-permute-start.6 = (bf16[2,2,128,128]{3,2,1,0:T(8,128)(2,1)S(1)}, bf16[2,2,128,128]{3,2,1,0:T(8,128)(2,1)S(1)}, u32[]{:S(2)}, u32[]{:S(2)}) collective-permute-start(bf16[2,2,128,128]{3,2,1,0:T(8,128)(2,1)S(1)} %get-tuple-element.192), channel_id=1, source_target_pairs={{0,1},{1,2},{2,3},{3,4},{4,5},{5,6},{6,7},{7,8},{8,9},{9,10},{10,1... | collective-permute-start | bytes 393224 | tf_op jit(solution)/shard_map/ppermute | solution.py:14
  31.3 33.1 %copy-start.3 = (bf16[1,1,12,128,128]{4,3,2,1,0:T(8,128)(2,1)S(1)}, bf16[1,1,12,128,128]{4,3,2,1,0:T(8,128)(2,1)}, u32[]{:S(2)}) copy-start(bf16[1,1,12,128,128]{4,3,2,1,0:T(8,128)(2,1)} %param.19) | copy-start | bytes 1179652
  31.3 12.1 %collective-permute-start.7 = (bf16[2,2,128,128]{3,2,1,0:T(8,128)(2,1)S(1)}, bf16[2,2,128,128]{3,2,1,0:T(8,128)(2,1)S(1)}, u32[]{:S(2)}, u32[]{:S(2)}) collective-permute-start(bf16[2,2,128,128]{3,2,1,0:T(8,128)(2,1)S(1)} %get-tuple-element.193), channel_id=1, source_target_pairs={{0,32},{32,64},{64,96},{96,128},{128,160},{160,192},{192,224},{224... | collective-permute-start | bytes 393224 | tf_op jit(solution)/shard_map/ppermute | solution.py:14
  37.0 11.9 %collective-permute-start.10 = (bf16[2,2,128,128]{3,2,1,0:T(8,128)(2,1)S(1)}, bf16[2,2,128,128]{3,2,1,0:T(8,128)(2,1)S(1)}, u32[]{:S(2)}, u32[]{:S(2)}) collective-permute-start(bf16[2,2,128,128]{3,2,1,0:T(8,128)(2,1)S(1)} %get-tuple-element.187), channel_id=1, source_target_pairs={{0,32},{32,64},{64,96},{96,128},{128,160},{160,192},{192,224},{224... | collective-permute-start | bytes 393224 | tf_op jit(solution)/shard_map/ppermute | solution.py:14
  41.3 13.3 %collective-permute-start.4 = (bf16[2,2,128,128]{3,2,1,0:T(8,128)(2,1)S(1)}, bf16[2,2,128,128]{3,2,1,0:T(8,128)(2,1)S(1)}, u32[]{:S(2)}, u32[]{:S(2)}) collective-permute-start(bf16[2,2,128,128]{3,2,1,0:T(8,128)(2,1)S(1)} %collective-permute-done.3), channel_id=1, source_target_pairs={{0,1},{1,2},{2,3},{3,4},{4,5},{5,6},{6,7},{7,8},{8,9},{9,10},{10,1... | collective-permute-start | bytes 393224 | tf_op jit(solution)/shard_map/ppermute | solution.py:14
  43.4 13.7 %collective-permute-start.9 = (bf16[2,2,128,128]{3,2,1,0:T(8,128)(2,1)S(1)}, bf16[2,2,128,128]{3,2,1,0:T(8,128)(2,1)S(1)}, u32[]{:S(2)}, u32[]{:S(2)}) collective-permute-start(bf16[2,2,128,128]{3,2,1,0:T(8,128)(2,1)S(1)} %get-tuple-element.194), channel_id=1, source_target_pairs={{0,32},{32,64},{64,96},{96,128},{128,160},{160,192},{192,224},{224... | collective-permute-start | bytes 393224 | tf_op jit(solution)/shard_map/ppermute | solution.py:14
  48.9 8.1 %collective-permute-start.8 = (bf16[2,2,128,128]{3,2,1,0:T(8,128)(2,1)S(1)}, bf16[2,2,128,128]{3,2,1,0:T(8,128)(2,1)S(1)}, u32[]{:S(2)}, u32[]{:S(2)}) collective-permute-start(bf16[2,2,128,128]{3,2,1,0:T(8,128)(2,1)S(1)} %collective-permute-done.7), channel_id=1, source_target_pairs={{1,0},{2,1},{3,2},{4,3},{5,4},{6,5},{7,6},{8,7},{9,8},{10,9},{11,1... | collective-permute-start | bytes 393224 | tf_op jit(solution)/shard_map/ppermute | solution.py:14
  54.5 8.9 %collective-permute-start.11 = (bf16[2,2,128,128]{3,2,1,0:T(8,128)(2,1)S(1)}, bf16[2,2,128,128]{3,2,1,0:T(8,128)(2,1)S(1)}, u32[]{:S(2)}, u32[]{:S(2)}) collective-permute-start(bf16[2,2,128,128]{3,2,1,0:T(8,128)(2,1)S(1)} %collective-permute-done.10), channel_id=1, source_target_pairs={{0,1},{1,2},{2,3},{3,4},{4,5},{5,6},{6,7},{7,8},{8,9},{9,10},{10,1... | collective-permute-start | bytes 393224 | tf_op jit(solution)/shard_map/ppermute | solution.py:14
  203.2 1.2 copy-start
  234.6 9.5 %copy-start.2 = (bf16[1,1,12,128,128]{4,3,2,1,0:T(8,128)(2,1)S(1)}, bf16[1,1,12,128,128]{4,3,2,1,0:T(8,128)(2,1)}, u32[]{:S(2)}) copy-start(bf16[1,1,12,128,128]{4,3,2,1,0:T(8,128)(2,1)} %param.18) | copy-start | bytes 1179652
  234.6 9.5 %copy-start.5 = (bf16[8,1,2,128,128]{4,3,2,1,0:T(8,128)(2,1)S(1)}, bf16[8,1,2,128,128]{4,3,2,1,0:T(8,128)(2,1)}, u32[]{:S(2)}) copy-start(bf16[8,1,2,128,128]{4,3,2,1,0:T(8,128)(2,1)} %get-tuple-element.186) | copy-start | bytes 1572868
  235.2 7.0 %collective-permute-start.12 = (bf16[2,128,128]{2,1,0:T(8,128)(2,1)S(1)}, bf16[2,128,128]{2,1,0:T(8,128)(2,1)S(1)}, u32[]{:S(2)}, u32[]{:S(2)}) collective-permute-start(bf16[2,128,128]{2,1,0:T(8,128)(2,1)S(1)} %bitcast.313), channel_id=1, source_target_pairs={{32,0},{64,32},{96,64},{128,96},{160,128},{192,160},{224,192},{256... | collective-permute-start | bytes 196616 | tf_op jit(solution)/shard_map/ppermute | solution.py:14
  236.5 18.7 %collective-permute-start.14 = (bf16[2,128,128]{2,1,0:T(8,128)(2,1)S(1)}, bf16[2,128,128]{2,1,0:T(8,128)(2,1)S(1)}, u32[]{:S(2)}, u32[]{:S(2)}) collective-permute-start(bf16[2,128,128]{2,1,0:T(8,128)(2,1)S(1)} %bitcast.306), channel_id=1, source_target_pairs={{32,0},{64,32},{96,64},{128,96},{160,128},{192,160},{224,192},{256... | collective-permute-start | bytes 196616 | tf_op jit(solution)/shard_map/ppermute | solution.py:14
  237.8 21.4 %collective-permute-start.15 = (bf16[2,128,128]{2,1,0:T(8,128)(2,1)S(1)}, bf16[2,128,128]{2,1,0:T(8,128)(2,1)S(1)}, u32[]{:S(2)}, u32[]{:S(2)}) collective-permute-start(bf16[2,128,128]{2,1,0:T(8,128)(2,1)S(1)} %bitcast.305), channel_id=1, source_target_pairs={{32,0},{64,32},{96,64},{128,96},{160,128},{192,160},{224,192},{256... | collective-permute-start | bytes 196616 | tf_op jit(solution)/shard_map/ppermute | solution.py:14
  242.2 9.3 %collective-permute-start.13 = (bf16[2,128,128]{2,1,0:T(8,128)(2,1)S(1)}, bf16[2,128,128]{2,1,0:T(8,128)(2,1)S(1)}, u32[]{:S(2)}, u32[]{:S(2)}) collective-permute-start(bf16[2,128,128]{2,1,0:T(8,128)(2,1)S(1)} %collective-permute-done.12), channel_id=1, source_target_pairs={{1,0},{2,1},{3,2},{4,3},{5,4},{6,5},{7,6},{8,7},{9,8},{10,9},{11,1... | collective-permute-start | bytes 196616 | tf_op jit(solution)/shard_map/ppermute | solution.py:14
  245.4 27.5 %collective-permute-start.17 = (bf16[2,128,128]{2,1,0:T(8,128)(2,1)S(1)}, bf16[2,128,128]{2,1,0:T(8,128)(2,1)S(1)}, u32[]{:S(2)}, u32[]{:S(2)}) collective-permute-start(bf16[2,128,128]{2,1,0:T(8,128)(2,1)S(1)} %bitcast.303), channel_id=1, source_target_pairs={{1,0},{2,1},{3,2},{4,3},{5,4},{6,5},{7,6},{8,7},{9,8},{10,9},{11,1... | collective-permute-start | bytes 196616 | tf_op jit(solution)/shard_map/ppermute | solution.py:14
  249.2 23.7 %collective-permute-start.18 = (bf16[2,128,128]{2,1,0:T(8,128)(2,1)S(1)}, bf16[2,128,128]{2,1,0:T(8,128)(2,1)S(1)}, u32[]{:S(2)}, u32[]{:S(2)}) collective-permute-start(bf16[2,128,128]{2,1,0:T(8,128)(2,1)S(1)} %bitcast.301), channel_id=1, source_target_pairs={{0,1},{1,2},{2,3},{3,4},{4,5},{5,6},{6,7},{7,8},{8,9},{9,10},{10,1... | collective-permute-start | bytes 196616 | tf_op jit(solution)/shard_map/ppermute | solution.py:14
  251.4 27.5 %copy-start.4 = (bf16[1,1,12,128,128]{4,3,2,1,0:T(8,128)(2,1)S(1)}, bf16[1,1,12,128,128]{4,3,2,1,0:T(8,128)(2,1)}, u32[]{:S(2)}) copy-start(bf16[1,1,12,128,128]{4,3,2,1,0:T(8,128)(2,1)} %param.19) | copy-start | bytes 1179652
  251.5 10.8 %collective-permute-start.19 = (bf16[2,128,128]{2,1,0:T(8,128)(2,1)S(1)}, bf16[2,128,128]{2,1,0:T(8,128)(2,1)S(1)}, u32[]{:S(2)}, u32[]{:S(2)}) collective-permute-start(bf16[2,128,128]{2,1,0:T(8,128)(2,1)S(1)} %bitcast.311), channel_id=1, source_target_pairs={{0,32},{32,64},{64,96},{96,128},{128,160},{160,192},{192,224},{224... | collective-permute-start | bytes 196616 | tf_op jit(solution)/shard_map/ppermute | solution.py:14
  255.3 11.1 %collective-permute-start.22 = (bf16[2,128,128]{2,1,0:T(8,128)(2,1)S(1)}, bf16[2,128,128]{2,1,0:T(8,128)(2,1)S(1)}, u32[]{:S(2)}, u32[]{:S(2)}) collective-permute-start(bf16[2,128,128]{2,1,0:T(8,128)(2,1)S(1)} %bitcast.309), channel_id=1, source_target_pairs={{0,32},{32,64},{64,96},{96,128},{128,160},{160,192},{192,224},{224... | collective-permute-start | bytes 196616 | tf_op jit(solution)/shard_map/ppermute | solution.py:14
  259.2 11.7 %collective-permute-start.16 = (bf16[2,128,128]{2,1,0:T(8,128)(2,1)S(1)}, bf16[2,128,128]{2,1,0:T(8,128)(2,1)S(1)}, u32[]{:S(2)}, u32[]{:S(2)}) collective-permute-start(bf16[2,128,128]{2,1,0:T(8,128)(2,1)S(1)} %collective-permute-done.15), channel_id=1, source_target_pairs={{0,1},{1,2},{2,3},{3,4},{4,5},{5,6},{6,7},{7,8},{8,9},{9,10},{10,1... | collective-permute-start | bytes 196616 | tf_op jit(solution)/shard_map/ppermute | solution.py:14
  262.3 10.6 %collective-permute-start.21 = (bf16[2,128,128]{2,1,0:T(8,128)(2,1)S(1)}, bf16[2,128,128]{2,1,0:T(8,128)(2,1)S(1)}, u32[]{:S(2)}, u32[]{:S(2)}) collective-permute-start(bf16[2,128,128]{2,1,0:T(8,128)(2,1)S(1)} %bitcast.299), channel_id=1, source_target_pairs={{0,32},{32,64},{64,96},{96,128},{128,160},{160,192},{192,224},{224... | collective-permute-start | bytes 196616 | tf_op jit(solution)/shard_map/ppermute | solution.py:14
  266.4 6.5 collective-permute-start.20
  270.9 8.0 %collective-permute-start.23 = (bf16[2,128,128]{2,1,0:T(8,128)(2,1)S(1)}, bf16[2,128,128]{2,1,0:T(8,128)(2,1)S(1)}, u32[]{:S(2)}, u32[]{:S(2)}) collective-permute-start(bf16[2,128,128]{2,1,0:T(8,128)(2,1)S(1)} %collective-permute-done.22), channel_id=1, source_target_pairs={{0,1},{1,2},{2,3},{3,4},{4,5},{5,6},{6,7},{7,8},{8,9},{9,10},{10,1... | collective-permute-start | bytes 196616 | tf_op jit(solution)/shard_map/ppermute | solution.py:14
  288.4 147.3 %copy-start.1 = (f32[27,128,128]{2,1,0:T(8,128)S(1)}, f32[27,128,128]{2,1,0:T(8,128)}, u32[]{:S(2)}) copy-start(f32[27,128,128]{2,1,0:T(8,128)} %copy-done) | copy-start | bytes 5308420
  439.3 216.8 %reduce-scatter.7.cloned.1.call-start = ((), (), s32[]{:S(2)}) async-start(), calls=%async_computation.2 | async-start | bytes 139264
  469.3 6.2 collective-permute-start.24
  475.4 9.8 %collective-permute-start.25 = (bf16[2,128,128]{2,1,0:T(8,128)(2,1)S(1)}, bf16[2,128,128]{2,1,0:T(8,128)(2,1)S(1)}, u32[]{:S(2)}, u32[]{:S(2)}) collective-permute-start(bf16[2,128,128]{2,1,0:T(8,128)(2,1)S(1)} %collective-permute-done.24), channel_id=1, source_target_pairs={{1,0},{2,1},{3,2},{4,3},{5,4},{6,5},{7,6},{8,7},{9,8},{10,9},{11,1... | collective-permute-start | bytes 196616 | tf_op jit(solution)/shard_map/ppermute | solution.py:14
  477.5 13.0 %collective-permute-start.26 = (bf16[2,128,128]{2,1,0:T(8,128)(2,1)S(1)}, bf16[2,128,128]{2,1,0:T(8,128)(2,1)S(1)}, u32[]{:S(2)}, u32[]{:S(2)}) collective-permute-start(bf16[2,128,128]{2,1,0:T(8,128)(2,1)S(1)} %bitcast.308), channel_id=1, source_target_pairs={{32,0},{64,32},{96,64},{128,96},{160,128},{192,160},{224,192},{256... | collective-permute-start | bytes 196616 | tf_op jit(solution)/shard_map/ppermute | solution.py:14
  478.8 15.4 %collective-permute-start.27 = (bf16[2,128,128]{2,1,0:T(8,128)(2,1)S(1)}, bf16[2,128,128]{2,1,0:T(8,128)(2,1)S(1)}, u32[]{:S(2)}, u32[]{:S(2)}) collective-permute-start(bf16[2,128,128]{2,1,0:T(8,128)(2,1)S(1)} %bitcast.307), channel_id=1, source_target_pairs={{32,0},{64,32},{96,64},{128,96},{160,128},{192,160},{224,192},{256... | collective-permute-start | bytes 196616 | tf_op jit(solution)/shard_map/ppermute | solution.py:14
  480.1 29.2 %collective-permute-start.29 = (bf16[2,128,128]{2,1,0:T(8,128)(2,1)S(1)}, bf16[2,128,128]{2,1,0:T(8,128)(2,1)S(1)}, u32[]{:S(2)}, u32[]{:S(2)}) collective-permute-start(bf16[2,128,128]{2,1,0:T(8,128)(2,1)S(1)} %bitcast.304), channel_id=1, source_target_pairs={{1,0},{2,1},{3,2},{4,3},{5,4},{6,5},{7,6},{8,7},{9,8},{10,9},{11,1... | collective-permute-start | bytes 196616 | tf_op jit(solution)/shard_map/ppermute | solution.py:14
  483.0 26.3 %collective-permute-start.30 = (bf16[2,128,128]{2,1,0:T(8,128)(2,1)S(1)}, bf16[2,128,128]{2,1,0:T(8,128)(2,1)S(1)}, u32[]{:S(2)}, u32[]{:S(2)}) collective-permute-start(bf16[2,128,128]{2,1,0:T(8,128)(2,1)S(1)} %bitcast.302), channel_id=1, source_target_pairs={{0,1},{1,2},{2,3},{3,4},{4,5},{5,6},{6,7},{7,8},{8,9},{9,10},{10,1... | collective-permute-start | bytes 196616 | tf_op jit(solution)/shard_map/ppermute | solution.py:14
  485.3 14.1 %collective-permute-start.31 = (bf16[2,128,128]{2,1,0:T(8,128)(2,1)S(1)}, bf16[2,128,128]{2,1,0:T(8,128)(2,1)S(1)}, u32[]{:S(2)}, u32[]{:S(2)}) collective-permute-start(bf16[2,128,128]{2,1,0:T(8,128)(2,1)S(1)} %bitcast.312), channel_id=1, source_target_pairs={{0,32},{32,64},{64,96},{96,128},{128,160},{160,192},{192,224},{224... | collective-permute-start | bytes 196616 | tf_op jit(solution)/shard_map/ppermute | solution.py:14
  490.5 13.0 %collective-permute-start.34 = (bf16[2,128,128]{2,1,0:T(8,128)(2,1)S(1)}, bf16[2,128,128]{2,1,0:T(8,128)(2,1)S(1)}, u32[]{:S(2)}, u32[]{:S(2)}) collective-permute-start(bf16[2,128,128]{2,1,0:T(8,128)(2,1)S(1)} %bitcast.310), channel_id=1, source_target_pairs={{0,32},{32,64},{64,96},{96,128},{128,160},{160,192},{192,224},{224... | collective-permute-start | bytes 196616 | tf_op jit(solution)/shard_map/ppermute | solution.py:14
  494.2 13.2 %collective-permute-start.28 = (bf16[2,128,128]{2,1,0:T(8,128)(2,1)S(1)}, bf16[2,128,128]{2,1,0:T(8,128)(2,1)S(1)}, u32[]{:S(2)}, u32[]{:S(2)}) collective-permute-start(bf16[2,128,128]{2,1,0:T(8,128)(2,1)S(1)} %collective-permute-done.27), channel_id=1, source_target_pairs={{0,1},{1,2},{2,3},{3,4},{4,5},{5,6},{6,7},{7,8},{8,9},{9,10},{10,1... | collective-permute-start | bytes 196616 | tf_op jit(solution)/shard_map/ppermute | solution.py:14
  499.4 10.0 %collective-permute-start.33 = (bf16[2,128,128]{2,1,0:T(8,128)(2,1)S(1)}, bf16[2,128,128]{2,1,0:T(8,128)(2,1)S(1)}, u32[]{:S(2)}, u32[]{:S(2)}) collective-permute-start(bf16[2,128,128]{2,1,0:T(8,128)(2,1)S(1)} %bitcast.300), channel_id=1, source_target_pairs={{0,32},{32,64},{64,96},{96,128},{128,160},{160,192},{192,224},{224... | collective-permute-start | bytes 196616 | tf_op jit(solution)/shard_map/ppermute | solution.py:14
  503.5 5.8 collective-permute-start.32
  507.3 75.1 %collective-permute-start.35 = (bf16[2,128,128]{2,1,0:T(8,128)(2,1)S(1)}, bf16[2,128,128]{2,1,0:T(8,128)(2,1)S(1)}, u32[]{:S(2)}, u32[]{:S(2)}) collective-permute-start(bf16[2,128,128]{2,1,0:T(8,128)(2,1)S(1)} %collective-permute-done.34), channel_id=1, source_target_pairs={{0,1},{1,2},{2,3},{3,4},{4,5},{5,6},{6,7},{7,8},{8,9},{9,10},{10,1... | collective-permute-start | bytes 196616 | tf_op jit(solution)/shard_map/ppermute | solution.py:14
Sparse Core Ops, SparseCore 0:
  439.4 141.2 reduce-scatter.8
  583.5 72.5 reduce-scatter.6
where the time goes:
time: 676 us; the launch traced here: 665 us
  local copies, waits for them, and re-layouts  229 us (34%)
  waiting for transfers between devices  171 us (25%)
  starting transfers between devices  105 us (16%)
  matrix products  90.2 us (13%)
  other arithmetic  51.2 us (8%)
  between operations  15.3 us (2%)
    unnamed x4, waiting for transfers between devices  143 us
    ppermute x36, starting transfers between devices, shifted(): lax.ppermute(value, axis, [(source, source + steps) for source in range(l...  105 us
    gather x54, local copies, waits for them, and re-layouts, per_offset(): sources = jnp.take(source_ext, in_row, axis=0).reshape(-1, channels)  96.1 us
    dot_general x54, matrix products, per_offset(): lax.dot_general(grad_rows, offset_weight, (((1,), (1,)), ((), ())), prefe...  52.3 us
    dynamic_update_slice x54, local copies, waits for them, and re-layouts, offsets_back(): lax.scan(per_offset, start, (weight, slot_in, slot_out))  46 us
    scatter-add x2, other arithmetic, offsets_back(): jax.ops.segment_sum(back_all, slot_in.reshape(-1), num_segments=ext_rows)  38.3 us
    dot_general x54, matrix products, per_offset(): lax.dot_general(sources, grad_rows, (((0,), (0,)), ((), ())), preferred_e...  36 us
    gather x54, local copies, waits for them, and re-layouts, per_offset(): grad_rows = jnp.take(grad_ext, out_row, axis=0).reshape(-1, channels)  31.9 us
  transfers between devices with their start and end apart: 38, of which 8 were waited for; matrix products, arithmetic and copies ran while one was open for 5% of the time, Pallas kernels for 0%

commit v1 on v0

v1 whole, which is shorter than its diff:
```python
import functools
import math

import jax
import jax.numpy as jnp
from jax import lax
from jax.experimental import pallas as pl
from jax.experimental.pallas import tpu as pltpu
from jax.sharding import PartitionSpec as P

HEADINGS = ((-1, -1), (-1, 0), (-1, 1), (0, -1), (0, 1), (1, -1), (1, 0), (1, 1))
KERNEL, MAP_CAP, BLOCKS, SEND_CAP, BLOCK = 27, 7, 12, 2, 128
HALO = 8 * SEND_CAP
ZERO = BLOCKS + HALO
SIDE = 14
MESH = pl.DeviceIdType.MESH
F32, BF16 = jnp.float32, jnp.bfloat16

T_IN = 0
T_OUT = T_IN + KERNEL * MAP_CAP
T_INV = T_OUT + KERNEL * MAP_CAP
T_BACK = T_INV + KERNEL * ZERO
T_SEND = T_BACK + 8 * BLOCKS
T_END = T_SEND + HALO


class Grid:
    def __init__(self, n_gx, n_gy, x_lo, x_hi):
        self.n_gx, self.n_gy, self.x_lo, self.x_hi = n_gx, n_gy, x_lo, x_hi
        self.z = n_gx // x_lo
        self.y = n_gy // (2 * x_hi)
        self.chips = n_gy // 2
        self.columns = 128 // n_gx
        self.rows = 2 * KERNEL * 128 // n_gy
        self.rows_pad = -(-self.rows // 256) * 256
        self.half = n_gy // 2
        self.quarter = n_gy // 4
        self.z_rows = 128 // self.z
        self.sources = x_lo * self.chips


def sigmoid(value):
    return 1.0 / (1.0 + jnp.exp(-value))


def kernel(grid, tab, feat, pre, cot, w1, w2, grad_out, weight_out, act_own, act_ext, feat_ext, g_ext, pg_ext,
           gt, acc, sb_act, sb_feat, sb_g, rb_g1, rb_g2, core_send, core_recv, own, z_send, z_recv, line,
           f_send, f_recv, halo_ssem, halo_rsem, core_ssem, core_rsem, z_ssem, z_rsem, f_ssem, f_rsem):
    gd = grid
    p, q = lax.axis_index("gx"), lax.axis_index("gy")
    z, xl = p % gd.z, p // gd.z
    core, chip_q = q % 2, q // 2

    barrier = pltpu.get_barrier_semaphore()

    def hello(px, qy):
        pl.semaphore_signal(barrier, inc=1, device_id=(px, qy), device_id_type=MESH)

    def hello_q(d, _):
        hello(p, (q + d) % gd.n_gy)
        return 0

    lax.fori_loop(1, gd.n_gy, hello_q, 0)
    greeted = gd.n_gy - 1
    for dx in range(1, gd.x_lo):
        other = ((xl + dx) % gd.x_lo) * gd.z + z

        def hello_x(d, _):
            hello(other, (q + d) % gd.n_gy)
            return 0

        lax.fori_loop(0, gd.n_gy, hello_x, 0)
        greeted += gd.n_gy
    for dz in range(1, gd.z):
        hello(xl * gd.z + (z + dz) % gd.z, q)
        greeted += 1
    for a, b in HEADINGS:
        if a != 0:
            hello((p + a + gd.n_gx) % gd.n_gx, (q + b + gd.n_gy) % gd.n_gy)
            greeted += 1

    zero_block = jnp.zeros((BLOCK, 128), BF16)
    act_ext[ZERO] = zero_block
    feat_ext[ZERO] = zero_block
    g_ext[BLOCKS] = zero_block
    pg_ext[BLOCKS] = zero_block
    gt[BLOCKS] = zero_block
    returned = (rb_g1, rb_g2)
    for buffer in returned:
        buffer[HALO] = zero_block

    def load_own(b, _):
        value = pre[b].astype(F32)
        value = (value * sigmoid(value)).astype(BF16)
        act_own[b] = value
        act_ext[b] = value
        feat_ext[b] = feat[b]
        g_ext[b] = cot[b]
        return 0

    lax.fori_loop(0, BLOCKS, load_own, 0)

    def pick(i, _):
        sb_act[i] = act_own[tab[T_SEND + i]]
        sb_feat[i] = feat[tab[T_SEND + i]]
        return 0

    lax.fori_loop(0, HALO, pick, 0)
    pl.semaphore_wait(barrier, greeted)

    def halo_copy(kind, e, src, dst, a, b):
        return pltpu.make_async_remote_copy(
            src_ref=src, dst_ref=dst, send_sem=halo_ssem.at[kind, e], recv_sem=halo_rsem.at[kind, e],
            device_id=((p + a + gd.n_gx) % gd.n_gx, (q + b + gd.n_gy) % gd.n_gy), device_id_type=MESH)

    def forth(kind, src, ext):
        return [halo_copy(kind, e, src.at[pl.ds(2 * e, 2)], ext.at[pl.ds(BLOCKS + 2 * e, 2)], a, b)
                for e, (a, b) in enumerate(HEADINGS)]

    def back(kind, layer):
        return [halo_copy(kind, e, sb_g.at[layer, pl.ds(2 * e, 2)], returned[layer].at[pl.ds(2 * e, 2)], -a, -b)
                for e, (a, b) in enumerate(HEADINGS)]

    def start(copies):
        for copy in copies:
            copy.start()

    def arrive(copies):
        for copy in copies:
            copy.wait_recv()

    act_copies, feat_copies = forth(0, sb_act, act_ext), forth(1, sb_feat, feat_ext)
    back_copies = [back(3, 0), back(2, 1)]
    start(act_copies)

    def products(grads, weight, j, n):
        lhs = jnp.concatenate(
            [jnp.concatenate([grads[tab[T_INV + k * ZERO + j + t]] for k in range(KERNEL)], axis=1)
             for t in range(n)], axis=0)
        rhs = jnp.concatenate([weight[k] for k in range(KERNEL)], axis=1)
        out = lax.dot_general(lhs, rhs, (((1,), (1,)), ((), ())), preferred_element_type=F32)
        return out.reshape(n, BLOCK, 128)

    def halo_partial(grads, weight, layer):
        def group(i, _):
            sb_g[layer, pl.ds(4 * i, 4)] = products(grads, weight, BLOCKS + 4 * i, 4).astype(BF16)
            return 0

        lax.fori_loop(0, HALO // 4, group, 0)

    def own_partial(grads, weight):
        def group(i, _):
            acc[pl.ds(4 * i, 4)] = products(grads, weight, 4 * i, 4)
            return 0

        lax.fori_loop(0, BLOCKS // 4, group, 0)

    def with_returned(b, layer):
        total = acc[b]
        for e in range(8):
            total = total + returned[layer][tab[T_BACK + e * BLOCKS + b]].astype(F32)
        return total

    def turn(grads):
        def one(b, _):
            t = grads[b].astype(F32).T
            step = gd.z * gd.columns
            t = jnp.concatenate(
                [t[x * step + c * gd.columns:x * step + (c + 1) * gd.columns]
                 for c in range(gd.z) for x in range(gd.x_lo)], axis=0)
            gt[b] = t.astype(BF16)
            return 0

        lax.fori_loop(0, BLOCKS, one, 0)

    def weight_term(sources, k):
        lhs = jnp.concatenate([gt[tab[T_OUT + k * MAP_CAP + m]] for m in range(MAP_CAP)], axis=1)
        rhs = jnp.concatenate([sources[tab[T_IN + k * MAP_CAP + m]] for m in range(MAP_CAP)], axis=0)
        return lax.dot_general(lhs, rhs, (((1,), (0,)), ((), ())), preferred_element_type=F32)

    def core_copy(layer):
        return pltpu.make_async_remote_copy(
            src_ref=core_send.at[layer], dst_ref=core_recv.at[layer], send_sem=core_ssem.at[layer],
            recv_sem=core_rsem.at[layer], device_id=(p, q + 1 - 2 * core), device_id_type=MESH)

    first_k = core * (KERNEL - SIDE)
    other_k = (1 - core) * (KERNEL - SIDE)
    core_copies = [core_copy(0), core_copy(1)]

    def weight_terms(sources, layer):
        def other(i, _):
            for u in range(7):
                core_send[layer, 7 * i + u] = weight_term(sources, other_k + 7 * i + u).astype(BF16)
            return 0

        lax.fori_loop(0, SIDE // 7, other, 0)
        core_copies[layer].start()

        def mine(i, _):
            for u in range(7):
                own[7 * i + u] = weight_term(sources, first_k + 7 * i + u)
            return 0

        lax.fori_loop(0, SIDE // 7, mine, 0)

    def z_copy(layer, dz):
        there = (z + dz) % gd.z
        return pltpu.make_async_remote_copy(
            src_ref=z_send.at[layer, there], dst_ref=z_recv.at[layer, dz], send_sem=z_ssem.at[layer, dz],
            recv_sem=z_rsem.at[layer, dz], device_id=(xl * gd.z + there, q), device_id_type=MESH)

    z_copies = [[z_copy(layer, dz) for dz in range(1, gd.z)] for layer in range(2)]

    def to_z(layer):
        core_copies[layer].wait_recv()

        def one(i, _):
            total = own[i] + core_recv[layer, i].astype(F32)
            total = total.astype(BF16)
            for c in range(gd.z):
                z_send[layer, c, i] = total[c * gd.z_rows:(c + 1) * gd.z_rows]
            return 0

        lax.fori_loop(0, SIDE, one, 0)
        start(z_copies[layer])

    source = xl * gd.chips + chip_q

    def f_copy(layer, slot, target):
        return pltpu.make_async_remote_copy(
            src_ref=f_send.at[layer, slot], dst_ref=f_recv.at[source], send_sem=f_ssem.at[layer, slot],
            recv_sem=f_rsem.at[source], device_id=target, device_id_type=MESH)

    def f_targets(layer):
        for x in range(gd.x_lo):
            for i in range(gd.quarter):
                target = (x * gd.z + z, layer * gd.half + core * gd.quarter + i)
                away = jnp.logical_or(target[0] != p, target[1] != q)
                yield x, i, x * gd.quarter + i, target, away

    def to_holders(layer):
        arrive(z_copies[layer])

        def one(i, _):
            total = z_send[layer, z, i].astype(F32)
            for dz in range(1, gd.z):
                total = total + z_recv[layer, dz, i].astype(F32)
            line[i] = total
            return 0

        lax.fori_loop(0, SIDE, one, 0)
        whole = jnp.concatenate([line[i] for i in range(SIDE)], axis=1)
        width = SIDE * 128
        shift = gd.rows * gd.quarter - (KERNEL - SIDE) * 128
        whole = jnp.where(core == 0, whole, pltpu.roll(whole, (width - shift) % width, 1))
        for i in range(gd.quarter):
            begin = i * gd.rows
            part = whole if begin == 0 else pltpu.roll(whole, width - begin, 1)
            part = part[:, :gd.rows_pad]
            half = gd.rows_pad // 2
            for x in range(gd.x_lo):
                chunk = part[x * gd.columns:(x + 1) * gd.columns]
                chunk = jnp.concatenate([chunk[:, :half], chunk[:, half:]], axis=0).astype(BF16)
                f_send[layer, x * gd.quarter + i] = chunk
        for x, i, slot, target, away in f_targets(layer):
            @pl.when(away)
            def _():
                f_copy(layer, slot, target).start()

            @pl.when(jnp.logical_not(away))
            def _():
                f_recv[source] = f_send[layer, slot]

    turn(g_ext)
    halo_partial(g_ext, w2, 1)
    start(back_copies[1])
    start(feat_copies)
    own_partial(g_ext, w2)
    arrive(act_copies)
    weight_terms(act_ext, 1)
    to_z(1)
    arrive(back_copies[1])

    def slope(b, _):
        value = pre[b].astype(F32)
        gate = sigmoid(value)
        pg_ext[b] = (with_returned(b, 1) * (gate * (1.0 + value * (1.0 - gate)))).astype(BF16)
        return 0

    lax.fori_loop(0, BLOCKS, slope, 0)
    turn(pg_ext)
    arrive(feat_copies)
    weight_terms(feat_ext, 0)
    to_z(0)
    halo_partial(pg_ext, w1, 0)
    start(back_copies[0])
    to_holders(1)
    own_partial(pg_ext, w1)
    to_holders(0)
    arrive(back_copies[0])

    def finish(b, _):
        grad_out[b] = with_returned(b, 0).astype(BF16)
        return 0

    lax.fori_loop(0, BLOCKS, finish, 0)

    sender_core = (q % gd.half) // gd.quarter

    def others(s, _):
        @pl.when(jnp.logical_not(jnp.logical_and(s == source, sender_core == core)))
        def _():
            pltpu.make_async_remote_copy(
                src_ref=f_send.at[0, 0], dst_ref=f_recv.at[s], send_sem=f_ssem.at[0, 0],
                recv_sem=f_rsem.at[s], device_id=(p, q + 1 - 2 * core), device_id_type=MESH).wait_recv()
        return 0

    lax.fori_loop(0, gd.sources, others, 0)
    total = f_recv[0].astype(F32)
    for s in range(1, gd.sources):
        total = total + f_recv[s].astype(F32)
    total = total * (1.0 / math.sqrt(MAP_CAP * BLOCK * gd.n_gx * gd.n_gy))
    total = jnp.concatenate([total[:gd.columns], total[gd.columns:]], axis=1)
    if gd.columns < 128:
        total = jnp.concatenate([total, jnp.zeros((128 - gd.columns, gd.rows_pad), F32)], axis=0)
    weight_out[...] = total.T[:gd.rows, :gd.columns]

    for copies in (act_copies, feat_copies, back_copies[0], back_copies[1], core_copies, z_copies[0], z_copies[1]):
        for copy in copies:
            copy.wait_send()
    for layer in range(2):
        for x, i, slot, target, away in f_targets(layer):
            @pl.when(away)
            def _():
                f_copy(layer, slot, target).wait_send()


def index_tables(grid, in_slots, out_slots, send_lists):
    p, q = lax.axis_index("gx"), lax.axis_index("gy")
    a = jnp.array([h[0] for h in HEADINGS], jnp.int32)
    b = jnp.array([h[1] for h in HEADINGS], jnp.int32)

    def inside(x, y):
        return (x >= 0) & (x < grid.n_gx) & (y >= 0) & (y < grid.n_gy)

    comes = inside(p - a, q - b)
    slot_heading = (in_slots - BLOCKS) // SEND_CAP
    missing = jnp.any((slot_heading[..., None] == jnp.arange(8)) & (in_slots[..., None] >= BLOCKS) & ~comes, axis=-1)
    read_slots = jnp.where(missing, ZERO, in_slots)
    slots = jnp.arange(ZERO, dtype=jnp.int32)
    inverse = jnp.min(jnp.where(in_slots[:, :, None] == slots, out_slots[:, :, None], BLOCKS), axis=1)
    returns = inside(p + a, q + b)
    own_blocks = jnp.arange(BLOCKS, dtype=jnp.int32)
    place = 2 * jnp.arange(8, dtype=jnp.int32)[:, None] + jnp.arange(SEND_CAP, dtype=jnp.int32)
    hit = (send_lists[:, :, None] == own_blocks) & returns[:, None, None]
    returned = jnp.min(jnp.where(hit, place[:, :, None], HALO), axis=1)
    parts = [read_slots, out_slots, inverse, returned, send_lists]
    return jnp.concatenate([part.reshape(-1) for part in parts])


def per_device(grid, features_in, pre_act, cotangent, w_first, w_second, in_slots, out_slots, send_lists):
    gd = grid
    table = index_tables(gd, in_slots[0, 0], out_slots[0, 0], send_lists[0, 0])
    ext = ZERO + 1
    half = gd.rows_pad // 2
    dma = pltpu.SemaphoreType.DMA
    block = (BLOCK, 128)
    vmem = pl.BlockSpec(memory_space=pltpu.VMEM)
    flops = 2 * 128 ** 3 * KERNEL * 2 * (ZERO + MAP_CAP)
    grad, weight = pl.pallas_call(
        functools.partial(kernel, gd),
        out_shape=(
            jax.ShapeDtypeStruct((BLOCKS,) + block, BF16),
            jax.ShapeDtypeStruct((gd.rows, gd.columns), F32),
        ),
        in_specs=[pl.BlockSpec(memory_space=pltpu.SMEM)] + [vmem] * 5,
        out_specs=(vmem, vmem),
        scratch_shapes=[
            pltpu.VMEM((BLOCKS,) + block, BF16),
            pltpu.VMEM((ext,) + block, BF16),
            pltpu.VMEM((ext,) + block, BF16),
            pltpu.VMEM((BLOCKS + 1,) + block, BF16),
            pltpu.VMEM((BLOCKS + 1,) + block, BF16),
            pltpu.VMEM((BLOCKS + 1,) + block, BF16),
            pltpu.VMEM((BLOCKS,) + block, F32),
            pltpu.VMEM((HALO,) + block, BF16),
            pltpu.VMEM((HALO,) + block, BF16),
            pltpu.VMEM((2, HALO) + block, BF16),
            pltpu.VMEM((HALO + 1,) + block, BF16),
            pltpu.VMEM((HALO + 1,) + block, BF16),
            pltpu.VMEM((2, SIDE) + block, BF16),
            pltpu.VMEM((2, SIDE) + block, BF16),
            pltpu.VMEM((SIDE,) + block, F32),
            pltpu.VMEM((2, gd.z, SIDE, gd.z_rows, 128), BF16),
            pltpu.VMEM((2, gd.z, SIDE, gd.z_rows, 128), BF16),
            pltpu.VMEM((SIDE, gd.z_rows, 128), F32),
            pltpu.VMEM((2, gd.x_lo * gd.quarter, 2 * gd.columns, half), BF16),
            pltpu.VMEM((gd.sources, 2 * gd.columns, half), BF16),
            dma((4, 8)),
            dma((4, 8)),
            dma((2,)),
            dma((2,)),
            dma((2, gd.z)),
            dma((2, gd.z)),
            dma((2, gd.x_lo * gd.quarter)),
            dma((gd.sources,)),
        ],
        compiler_params=pltpu.CompilerParams(
            collective_id=0, has_side_effects=True, vmem_limit_bytes=40 * 1024 * 1024
        ),
        cost_estimate=pl.CostEstimate(flops=flops, bytes_accessed=8 * 2 ** 20, transcendentals=0),
    )(table, features_in[0, 0], pre_act[0, 0], cotangent[0, 0], w_first, w_second)
    return grad[None, None], weight


def build(mesh, x_lo, x_hi):
    grid = Grid(mesh.shape["gx"], mesh.shape["gy"], x_lo, x_hi)
    in_specs = (
        P("gx", "gy", None, None, None),
        P("gx", "gy", None, None, None),
        P("gx", "gy", None, None, None),
        P(),
        P(),
        P("gx", "gy", None, None),
        P("gx", "gy", None, None),
        P("gx", "gy", None, None),
    )
    out_specs = (P("gx", "gy", None, None, None), P("gy", "gx"))
    return jax.shard_map(
        functools.partial(per_device, grid), mesh=mesh, in_specs=in_specs, out_specs=out_specs, check_vma=False
    )


def solution(mesh):
    return build(mesh, 2, 2)
```

time: 676 us -> 77.6 us (0.11)
  the two profiles are of different devices: /device:TPU:24 before, /device:TPU:1 now
where the time goes in v1:
time: 77.6 us; the launch traced here: 77.2 us
  Pallas kernels  65.6 us (85%)
  local copies, waits for them, and re-layouts  10.4 us (13%)
    pallas_call x1, Pallas kernels, per_device(): pl.pallas_call(functools.partial(kernel, gd), out_shape=(jax.ShapeDtypeSt...  65.6 us
    unnamed x30, local copies, waits for them, and re-layouts  9.69 us

profile of v1, /device:TPU:1, one launch (start us, length us, event | category | flops | bytes accessed | tf_op | source)
XLA Modules:
  0.0 77.2 jit_solution(17752546830281486062)
XLA Ops:
  0.6 0.0 copy-start.11
  0.6 0.0 copy-start.8
  0.7 0.0 copy-start.9
  0.7 0.0 copy-start.10
  0.7 0.6 copy-done.11
  1.3 0.0 copy-done.8
  1.3 0.0 copy-done.9
  1.3 0.0 copy-done.10
  1.4 0.0 copy-start.5
  1.4 0.7 copy-done.5
  2.0 0.0 copy-start.6
  2.0 0.7 copy-done.6
  2.7 0.1 select_reduce_fusion.1
  2.8 0.1 reshape.71
  2.9 0.1 copy.33
  3.0 0.1 reshape_squeeze.7
  3.1 0.1 fusion.2
  3.2 0.1 copy.28
  3.3 0.0 copy-start.7
  3.3 0.1 reduce_or.12
  3.4 0.6 copy-done.7
  4.0 0.1 copy.30
  4.1 0.1 reshape_squeeze.6
  4.2 0.1 copy.29
  4.3 0.1 squeeze.15
  4.4 0.1 copy.37
  4.5 0.1 select_reduce_fusion
  4.6 0.1 reshape.70
  4.7 0.1 concatenate.3.tab
  4.8 0.0 copy-start
  4.8 1.2 %copy-done = bf16[27,128,128]{2,1,0:T(8,128)(2,1)S(1)} copy-done((bf16[27,128,128]{2,1,0:T(8,128)(2,1)S(1)}, bf16[27,128,128]{2,1,0:T(8,128)(2,1)}, u32[]{:S(2)}) %copy-start) | copy-done | bytes 884760
  6.0 0.0 copy-start.1
  6.0 1.2 %copy-done.1 = bf16[27,128,128]{2,1,0:T(8,128)(2,1)S(1)} copy-done((bf16[27,128,128]{2,1,0:T(8,128)(2,1)S(1)}, bf16[27,128,128]{2,1,0:T(8,128)(2,1)}, u32[]{:S(2)}) %copy-start.1) | copy-done | bytes 884760
  7.1 0.0 copy-start.2
  7.1 1.0 %copy-done.2 = bf16[1,1,12,128,128]{4,3,2,1,0:T(8,128)(2,1)S(1)} copy-done((bf16[1,1,12,128,128]{4,3,2,1,0:T(8,128)(2,1)S(1)}, bf16[1,1,12,128,128]{4,3,2,1,0:T(8,128)(2,1)}, u32[]{:S(2)}) %copy-start.2) | copy-done | bytes 393240
  8.1 0.0 copy-start.3
  8.1 1.0 %copy-done.3 = bf16[1,1,12,128,128]{4,3,2,1,0:T(8,128)(2,1)S(1)} copy-done((bf16[1,1,12,128,128]{4,3,2,1,0:T(8,128)(2,1)S(1)}, bf16[1,1,12,128,128]{4,3,2,1,0:T(8,128)(2,1)}, u32[]{:S(2)}) %copy-start.3) | copy-done | bytes 393240
  9.1 0.0 copy-start.4
  9.1 1.0 %copy-done.4 = bf16[1,1,12,128,128]{4,3,2,1,0:T(8,128)(2,1)S(1)} copy-done((bf16[1,1,12,128,128]{4,3,2,1,0:T(8,128)(2,1)S(1)}, bf16[1,1,12,128,128]{4,3,2,1,0:T(8,128)(2,1)}, u32[]{:S(2)}) %copy-start.4) | copy-done | bytes 393240
  10.1 65.6 %shard_map.113 = (bf16[12,128,128]{2,1,0:T(8,128)(2,1)S(1)}, f32[216,8]{1,0:T(8,128)S(1)}) custom-call(s32[1246]{0:T(1024)S(1)} %concatenate.3.tab, bf16[12,128,128]{2,1,0:T(8,128)(2,1)S(1)} %bitcast.15, bf16[12,128,128]{2,1,0:T(8,128)(2,1)S(1)} %bitcast.16, bf16[12,128,128]{2,1,0:T(8,128)(2,1)S(1)} %bitcast.17, bf16[27,128,128]{2,1,0:T(8,128)(2,1)S(1)} %copy-done, ...), custom_call_target="tpu_custom_call" | custom-call | flops 7927234560 | bytes 8388608 | tf_op jit(solution)/shard_map/pallas_call | solution.py:370
  75.8 0.7 copy.34
  76.4 0.7 copy.43
  (6 shorter events, 0.0 us)
Async XLA Ops:
  0.6 0.7 copy-start.11
  0.6 0.7 copy-start.8
  0.7 0.7 copy-start.9
  0.7 0.7 copy-start.10
  1.4 0.7 copy-start.5
  2.0 0.7 copy-start.6
  3.3 0.7 copy-start.7
  4.8 1.2 %copy-start = (bf16[27,128,128]{2,1,0:T(8,128)(2,1)S(1)}, bf16[27,128,128]{2,1,0:T(8,128)(2,1)}, u32[]{:S(2)}) copy-start(bf16[27,128,128]{2,1,0:T(8,128)(2,1)} %w1.1) | copy-start | bytes 2654212
  6.0 1.2 %copy-start.1 = (bf16[27,128,128]{2,1,0:T(8,128)(2,1)S(1)}, bf16[27,128,128]{2,1,0:T(8,128)(2,1)}, u32[]{:S(2)}) copy-start(bf16[27,128,128]{2,1,0:T(8,128)(2,1)} %w2.1) | copy-start | bytes 2654212
  7.1 1.0 %copy-start.2 = (bf16[1,1,12,128,128]{4,3,2,1,0:T(8,128)(2,1)S(1)}, bf16[1,1,12,128,128]{4,3,2,1,0:T(8,128)(2,1)}, u32[]{:S(2)}) copy-start(bf16[1,1,12,128,128]{4,3,2,1,0:T(8,128)(2,1)} %param.10) | copy-start | bytes 1179652
  8.1 1.0 %copy-start.3 = (bf16[1,1,12,128,128]{4,3,2,1,0:T(8,128)(2,1)S(1)}, bf16[1,1,12,128,128]{4,3,2,1,0:T(8,128)(2,1)}, u32[]{:S(2)}) copy-start(bf16[1,1,12,128,128]{4,3,2,1,0:T(8,128)(2,1)} %param.11) | copy-start | bytes 1179652
  9.1 1.0 %copy-start.4 = (bf16[1,1,12,128,128]{4,3,2,1,0:T(8,128)(2,1)S(1)}, bf16[1,1,12,128,128]{4,3,2,1,0:T(8,128)(2,1)}, u32[]{:S(2)}) copy-start(bf16[1,1,12,128,128]{4,3,2,1,0:T(8,128)(2,1)} %param.12) | copy-start | bytes 1179652

commit v2 on v1

v2 whole, which is shorter than its diff:
```python
import functools
import math

import jax
import jax.numpy as jnp
from jax import lax
from jax.experimental import pallas as pl
from jax.experimental.pallas import tpu as pltpu
from jax.sharding import PartitionSpec as P

HEADINGS = ((-1, -1), (-1, 0), (-1, 1), (0, -1), (0, 1), (1, -1), (1, 0), (1, 1))
KERNEL, MAP_CAP, BLOCKS, SEND_CAP, BLOCK = 27, 7, 12, 2, 128
HALO = 8 * SEND_CAP
ZERO = BLOCKS + HALO
SIDE = 14
MESH = pl.DeviceIdType.MESH
F32, BF16 = jnp.float32, jnp.bfloat16

class Grid:
    def __init__(self, n_gx, n_gy, x_lo, x_hi):
        self.n_gx, self.n_gy, self.x_lo, self.x_hi = n_gx, n_gy, x_lo, x_hi
        self.z = n_gx // x_lo
        self.y = n_gy // (2 * x_hi)
        self.chips = n_gy // 2
        self.columns = 128 // n_gx
        self.rows = 2 * KERNEL * 128 // n_gy
        self.rows_pad = -(-self.rows // 256) * 256
        self.half = n_gy // 2
        self.quarter = n_gy // 4
        self.ring = self.z
        self.sources = x_lo * x_hi * self.ring


def sigmoid(value):
    return 1.0 / (1.0 + jnp.exp(-value))


def kernel(grid, in_hbm, out_hbm, send_hbm, feat_hbm, pre_hbm, cot_hbm, w1_hbm, w2_hbm, grad_hbm, weight_out,
           in_vec, out_vec, inv_vec, in_tab, out_tab, send_tab, inv_tab, feat, pre, w1, w2, grad_out,
           act_own, act_ext, feat_ext, g_ext, pg_ext, gt, acc, sb_act, sb_feat, sb_g, rb_g1, rb_g2,
           core_send, core_recv, own, r_send, r_recv, line, f_send, f_recv,
           load_sem, halo_ssem, halo_rsem, core_ssem, core_rsem, r_ssem, r_rsem, f_ssem, f_rsem):
    gd = grid
    p, q = lax.axis_index("gx"), lax.axis_index("gy")
    z, xl = p % gd.z, p // gd.z
    core, chip_q = q % 2, q // 2
    y, xh = chip_q // gd.x_hi, chip_q % gd.x_hi

    def load(n, src, dst):
        copy = pltpu.make_async_copy(src, dst, load_sem.at[n])
        copy.start()
        return copy

    got_in = load(0, in_hbm, in_vec)
    got_out = load(1, out_hbm, out_vec)
    got_send = load(2, send_hbm, send_tab)
    got_pre = load(3, pre_hbm, pre)
    got_feat = load(4, feat_hbm, feat)
    got_cot = load(5, cot_hbm, g_ext.at[pl.ds(0, BLOCKS)])
    got_w2 = load(6, w2_hbm, w2)
    got_in_tab = load(7, in_hbm, in_tab)
    got_out_tab = load(8, out_hbm, out_tab)
    got_feat_ext = load(9, feat_hbm, feat_ext.at[pl.ds(0, BLOCKS)])
    got_w1 = load(10, w1_hbm, w1)

    barrier = pltpu.get_barrier_semaphore()

    def hello(px, qy):
        pl.semaphore_signal(barrier, inc=1, device_id=(px, qy), device_id_type=MESH)

    sender_core = (q % gd.half) // gd.quarter

    def hello_source(s, _):
        x, i = s // gd.ring, s % gd.ring
        px = jnp.where(xl == 0, (x // gd.x_hi) * gd.z + i, (x // gd.x_hi) * gd.z + z)
        qy = (jnp.where(xl == 0, z, i) * gd.x_hi + x % gd.x_hi) * 2 + sender_core
        hello(px, qy)
        return 0

    lax.fori_loop(0, gd.sources, hello_source, 0)
    for d in range(1, gd.ring):
        hello(xl * gd.z + (z + d) % gd.z, q)
        hello(p, (((y + d) % gd.y) * gd.x_hi + xh) * 2 + core)
    hello(p, q + 1 - 2 * core)
    for a, b in HEADINGS:
        hello((p + a + gd.n_gx) % gd.n_gx, (q + b + gd.n_gy) % gd.n_gy)
    greeted = 2 * gd.x_lo * gd.quarter + 2 * (gd.ring - 1) + 1 + 8

    zero_block = jnp.zeros((BLOCK, 128), BF16)
    returned = (rb_g1, rb_g2)
    for buffer, place in ((act_ext, ZERO), (feat_ext, ZERO), (g_ext, BLOCKS), (pg_ext, BLOCKS), (gt, BLOCKS),
                          (rb_g1, HALO), (rb_g2, HALO)):
        buffer[place] = zero_block

    got_in.wait()
    got_out.wait()
    inv_vec[...] = jnp.zeros(inv_vec.shape, jnp.int32)
    slots = lax.broadcasted_iota(jnp.int32, (ZERO, KERNEL), 0)
    inverse = jnp.full((ZERO, KERNEL), BLOCKS, jnp.int32)
    for m in range(MAP_CAP):
        inverse = jnp.where(in_vec[m] == slots, out_vec[m], inverse)
    inv_vec[:ZERO, :KERNEL] = inverse
    got_inv = load(11, inv_vec, inv_tab)

    got_pre.wait()

    def load_own(b, _):
        value = pre[b].astype(F32)
        value = (value * sigmoid(value)).astype(BF16)
        act_own[b] = value
        act_ext[b] = value
        return 0

    lax.fori_loop(0, BLOCKS, load_own, 0)
    got_send.wait()
    got_feat.wait()

    def pick(e, _):
        for s in range(SEND_CAP):
            sb_act[2 * e + s] = act_own[send_tab[s, e]]
            sb_feat[2 * e + s] = feat[send_tab[s, e]]
        return 0

    lax.fori_loop(0, 8, pick, 0)

    def halo_copy(kind, e, src, dst, a, b):
        return pltpu.make_async_remote_copy(
            src_ref=src, dst_ref=dst, send_sem=halo_ssem.at[kind, e], recv_sem=halo_rsem.at[kind, e],
            device_id=((p + a + gd.n_gx) % gd.n_gx, (q + b + gd.n_gy) % gd.n_gy), device_id_type=MESH)

    def forth(kind, src, ext):
        return [halo_copy(kind, e, src.at[pl.ds(2 * e, 2)], ext.at[pl.ds(BLOCKS + 2 * e, 2)], a, b)
                for e, (a, b) in enumerate(HEADINGS)]

    def back(kind, layer):
        return [halo_copy(kind, e, sb_g.at[layer, pl.ds(2 * e, 2)], returned[layer].at[pl.ds(2 * e, 2)], -a, -b)
                for e, (a, b) in enumerate(HEADINGS)]

    def start(copies):
        for copy in copies:
            copy.start()

    def arrive(copies):
        for copy in copies:
            copy.wait_recv()

    def arrive_halo(copies, buffer, first, sign):
        arrive(copies)
        for e, (a, b) in enumerate(HEADINGS):
            px, qy = p + sign * a, q + sign * b
            inside = (px >= 0) & (px < gd.n_gx) & (qy >= 0) & (qy < gd.n_gy)

            @pl.when(jnp.logical_not(inside))
            def _():
                for s in range(SEND_CAP):
                    buffer[first + 2 * e + s] = zero_block

    act_copies, feat_copies = forth(0, sb_act, act_ext), forth(1, sb_feat, feat_ext)
    back_copies = [back(3, 0), back(2, 1)]

    def products(grads, weight, j, n):
        lhs = jnp.concatenate(
            [jnp.concatenate([grads[inv_tab[j + t, k]] for k in range(KERNEL)], axis=1) for t in range(n)], axis=0)
        rhs = jnp.concatenate([weight[k] for k in range(KERNEL)], axis=1)
        out = lax.dot_general(lhs, rhs, (((1,), (1,)), ((), ())), preferred_element_type=F32)
        return out.reshape(n, BLOCK, 128)

    def halo_partial(grads, weight, layer):
        def group(i, _):
            sb_g[layer, pl.ds(4 * i, 4)] = products(grads, weight, BLOCKS + 4 * i, 4).astype(BF16)
            return 0

        lax.fori_loop(0, HALO // 4, group, 0)

    def own_partial(grads, weight):
        def group(i, _):
            acc[pl.ds(4 * i, 4)] = products(grads, weight, 4 * i, 4)
            return 0

        lax.fori_loop(0, BLOCKS // 4, group, 0)

    def with_returned(b, layer):
        total = acc[b]
        for e in range(8):
            place = jnp.where(send_tab[0, e] == b, 2 * e, jnp.where(send_tab[1, e] == b, 2 * e + 1, HALO))
            total = total + returned[layer][place].astype(F32)
        return total

    def turn(grads):
        def one(b, _):
            gt[b] = grads[b].T
            return 0

        lax.fori_loop(0, BLOCKS, one, 0)

    def weight_term(sources, k):
        lhs = jnp.concatenate([gt[out_tab[m, 0, k]] for m in range(MAP_CAP)], axis=1)
        rhs = jnp.concatenate([sources[in_tab[m, 0, k]] for m in range(MAP_CAP)], axis=0)
        return lax.dot_general(lhs, rhs, (((1,), (0,)), ((), ())), preferred_element_type=F32)

    def core_copy(layer):
        return pltpu.make_async_remote_copy(
            src_ref=core_send.at[layer], dst_ref=core_recv.at[layer], send_sem=core_ssem.at[layer],
            recv_sem=core_rsem.at[layer], device_id=(p, q + 1 - 2 * core), device_id_type=MESH)

    first_k = core * (KERNEL - SIDE)
    other_k = (1 - core) * (KERNEL - SIDE)
    core_copies = [core_copy(0), core_copy(1)]

    def weight_terms(sources, layer):
        def other(i, _):
            for u in range(7):
                core_send[layer, 7 * i + u] = weight_term(sources, other_k + 7 * i + u).astype(BF16)
            return 0

        lax.fori_loop(0, SIDE // 7, other, 0)
        core_copies[layer].start()

        def mine(i, _):
            for u in range(7):
                own[7 * i + u] = weight_term(sources, first_k + 7 * i + u)
            return 0

        lax.fori_loop(0, SIDE // 7, mine, 0)

    def ring_copy(layer, x, d):
        if x == 0:
            there = (y + d) % gd.y
            target = (p, (there * gd.x_hi + xh) * 2 + core)
        else:
            there = (z + d) % gd.z
            target = (xl * gd.z + there, q)
        return pltpu.make_async_remote_copy(
            src_ref=r_send.at[layer, x, there], dst_ref=r_recv.at[layer, x, d], send_sem=r_ssem.at[layer, x, d],
            recv_sem=r_rsem.at[layer, x, d], device_id=target, device_id_type=MESH)

    ring_copies = [[[ring_copy(layer, x, d) for d in range(1, gd.ring)] for x in range(gd.x_lo)] for layer in range(2)]

    def to_rings(layer):
        core_copies[layer].wait_recv()

        def one(i, _):
            low = own[i] + core_recv[layer, i].astype(F32)
            high = own[i + SIDE // 2] + core_recv[layer, i + SIDE // 2].astype(F32)
            for x in range(gd.x_lo):
                for c in range(gd.ring):
                    rows = slice((x * gd.ring + c) * gd.columns, (x * gd.ring + c + 1) * gd.columns)
                    r_send[layer, x, c, i] = jnp.concatenate([low[rows], high[rows]], axis=0).astype(BF16)
            return 0

        lax.fori_loop(0, SIDE // 2, one, 0)
        for x in range(gd.x_lo):
            start(ring_copies[layer][x])

    places = [(xl * gd.x_hi + xh) * gd.ring + z, (xl * gd.x_hi + xh) * gd.ring + y]

    def f_copy(layer, x, i):
        column = y if x == 0 else z
        target = (x * gd.z + column, layer * gd.half + core * gd.quarter + i)
        slot = x * gd.quarter + i
        copy = pltpu.make_async_remote_copy(
            src_ref=f_send.at[layer, slot], dst_ref=f_recv.at[places[x]], send_sem=f_ssem.at[layer, slot],
            recv_sem=f_rsem.at[places[x]], device_id=target, device_id_type=MESH)
        return copy, jnp.logical_or(target[0] != p, target[1] != q)

    def to_holders(layer):
        width = SIDE * 128
        half = gd.rows_pad // 2
        for x in range(gd.x_lo):
            arrive(ring_copies[layer][x])
            mine = y if x == 0 else z

            def one(i, _):
                total = r_send[layer, x, mine, i].astype(F32)
                for d in range(1, gd.ring):
                    total = total + r_recv[layer, x, d, i].astype(F32)
                line[i] = total
                return 0

            lax.fori_loop(0, SIDE // 2, one, 0)
            whole = jnp.concatenate(
                [line[i, h * gd.columns:(h + 1) * gd.columns] for h in range(2) for i in range(SIDE // 2)], axis=1)
            shift = gd.rows * gd.quarter - (KERNEL - SIDE) * 128
            whole = jnp.where(core == 0, whole, pltpu.roll(whole, (width - shift) % width, 1))
            for i in range(gd.quarter):
                begin = i * gd.rows
                part = whole if begin == 0 else pltpu.roll(whole, width - begin, 1)
                chunk = jnp.concatenate([part[:, :half], part[:, half:gd.rows_pad]], axis=0)
                f_send[layer, x * gd.quarter + i] = chunk.astype(BF16)
            for i in range(gd.quarter):
                copy, away = f_copy(layer, x, i)

                @pl.when(away)
                def _():
                    copy.start()

                @pl.when(jnp.logical_not(away))
                def _():
                    f_recv[places[x]] = f_send[layer, x * gd.quarter + i]

    pl.semaphore_wait(barrier, greeted)
    start(act_copies)
    got_cot.wait()
    got_w2.wait()
    got_inv.wait()
    halo_partial(g_ext, w2, 1)
    start(back_copies[1])
    start(feat_copies)
    turn(g_ext)
    own_partial(g_ext, w2)
    got_in_tab.wait()
    got_out_tab.wait()
    arrive_halo(act_copies, act_ext, BLOCKS, -1)
    weight_terms(act_ext, 1)
    to_rings(1)
    arrive_halo(back_copies[1], rb_g2, 0, 1)

    def slope(b, _):
        value = pre[b].astype(F32)
        gate = sigmoid(value)
        pg_ext[b] = (with_returned(b, 1) * (gate * (1.0 + value * (1.0 - gate)))).astype(BF16)
        return 0

    lax.fori_loop(0, BLOCKS, slope, 0)
    turn(pg_ext)
    got_feat_ext.wait()
    got_w1.wait()
    arrive_halo(feat_copies, feat_ext, BLOCKS, -1)
    weight_terms(feat_ext, 0)
    to_rings(0)
    halo_partial(pg_ext, w1, 0)
    start(back_copies[0])
    to_holders(1)
    own_partial(pg_ext, w1)
    to_holders(0)
    arrive_halo(back_copies[0], rb_g1, 0, 1)

    def finish(b, _):
        grad_out[b] = with_returned(b, 0).astype(BF16)
        return 0

    lax.fori_loop(0, BLOCKS, finish, 0)
    stored = load(12, grad_out, grad_hbm)

    own_place = jnp.where(xl == 0, places[0], places[1])
    holds_own = jnp.logical_and(sender_core == core, jnp.where(xl == 0, y, z) == z)

    def others(s, _):
        @pl.when(jnp.logical_not(jnp.logical_and(s == own_place, holds_own)))
        def _():
            pltpu.make_async_remote_copy(
                src_ref=f_send.at[0, 0], dst_ref=f_recv.at[s], send_sem=f_ssem.at[0, 0],
                recv_sem=f_rsem.at[s], device_id=(p, q + 1 - 2 * core), device_id_type=MESH).wait_recv()
        return 0

    lax.fori_loop(0, gd.sources, others, 0)
    total = f_recv[0].astype(F32)
    for s in range(1, gd.sources):
        total = total + f_recv[s].astype(F32)
    total = total * (1.0 / math.sqrt(MAP_CAP * BLOCK * gd.n_gx * gd.n_gy))
    total = jnp.concatenate([total[:gd.columns], total[gd.columns:]], axis=1)
    weight_out[...] = total[:, :gd.rows]

    for copies in [act_copies, feat_copies, core_copies] + back_copies + ring_copies[0] + ring_copies[1]:
        for copy in copies:
            copy.wait_send()
    for layer in range(2):
        for x in range(gd.x_lo):
            for i in range(gd.quarter):
                copy, away = f_copy(layer, x, i)

                @pl.when(away)
                def _():
                    copy.wait_send()
    stored.wait()


def per_device(grid, features_in, pre_act, cotangent, w_first, w_second, in_slots, out_slots, send_lists):
    gd = grid
    slots_in = jnp.transpose(in_slots[0], (2, 0, 1))
    slots_out = jnp.transpose(out_slots[0], (2, 0, 1))
    sends = jnp.transpose(send_lists[0, 0])
    ext = ZERO + 1
    half = gd.rows_pad // 2
    dma = pltpu.SemaphoreType.DMA
    block = (BLOCK, 128)
    slots = (MAP_CAP, 1, KERNEL)
    hbm = pl.BlockSpec(memory_space=pltpu.HBM)
    flops = 2 * 128 ** 3 * KERNEL * 2 * (ZERO + MAP_CAP)
    grad, weight = pl.pallas_call(
        functools.partial(kernel, gd),
        out_shape=(
            jax.ShapeDtypeStruct((BLOCKS,) + block, BF16),
            jax.ShapeDtypeStruct((gd.columns, gd.rows), F32),
        ),
        in_specs=[hbm] * 8,
        out_specs=(hbm, pl.BlockSpec(memory_space=pltpu.VMEM)),
        scratch_shapes=[
            pltpu.VMEM(slots, jnp.int32),
            pltpu.VMEM(slots, jnp.int32),
            pltpu.VMEM((32, 128), jnp.int32),
            pltpu.SMEM(slots, jnp.int32),
            pltpu.SMEM(slots, jnp.int32),
            pltpu.SMEM((SEND_CAP, 8), jnp.int32),
            pltpu.SMEM((32, 128), jnp.int32),
            pltpu.VMEM((BLOCKS,) + block, BF16),
            pltpu.VMEM((BLOCKS,) + block, BF16),
            pltpu.VMEM((KERNEL,) + block, BF16),
            pltpu.VMEM((KERNEL,) + block, BF16),
            pltpu.VMEM((BLOCKS,) + block, BF16),
            pltpu.VMEM((BLOCKS,) + block, BF16),
            pltpu.VMEM((ext,) + block, BF16),
            pltpu.VMEM((ext,) + block, BF16),
            pltpu.VMEM((BLOCKS + 1,) + block, BF16),
            pltpu.VMEM((BLOCKS + 1,) + block, BF16),
            pltpu.VMEM((BLOCKS + 1,) + block, BF16),
            pltpu.VMEM((BLOCKS,) + block, F32),
            pltpu.VMEM((HALO,) + block, BF16),
            pltpu.VMEM((HALO,) + block, BF16),
            pltpu.VMEM((2, HALO) + block, BF16),
            pltpu.VMEM((HALO + 1,) + block, BF16),
            pltpu.VMEM((HALO + 1,) + block, BF16),
            pltpu.VMEM((2, SIDE) + block, BF16),
            pltpu.VMEM((2, SIDE) + block, BF16),
            pltpu.VMEM((SIDE,) + block, F32),
            pltpu.VMEM((2, gd.x_lo, gd.ring, SIDE // 2, 2 * gd.columns, 128), BF16),
            pltpu.VMEM((2, gd.x_lo, gd.ring, SIDE // 2, 2 * gd.columns, 128), BF16),
            pltpu.VMEM((SIDE // 2, 2 * gd.columns, 128), F32),
            pltpu.VMEM((2, gd.x_lo * gd.quarter, 2 * gd.columns, half), BF16),
            pltpu.VMEM((gd.sources, 2 * gd.columns, half), BF16),
            dma((13,)),
            dma((4, 8)),
            dma((4, 8)),
            dma((2,)),
            dma((2,)),
            dma((2, gd.x_lo, gd.ring)),
            dma((2, gd.x_lo, gd.ring)),
            dma((2, gd.x_lo * gd.quarter)),
            dma((gd.sources,)),
        ],
        compiler_params=pltpu.CompilerParams(
            collective_id=0, has_side_effects=True, vmem_limit_bytes=56 * 1024 * 1024
        ),
        cost_estimate=pl.CostEstimate(flops=flops, bytes_accessed=8 * 2 ** 20, transcendentals=0),
    )(slots_in, slots_out, sends, features_in[0, 0], pre_act[0, 0], cotangent[0, 0], w_first, w_second)
    return grad[None, None], weight.T


def build(mesh, x_lo, x_hi):
    grid = Grid(mesh.shape["gx"], mesh.shape["gy"], x_lo, x_hi)
    in_specs = (
        P("gx", "gy", None, None, None),
        P("gx", "gy", None, None, None),
        P("gx", "gy", None, None, None),
        P(),
        P(),
        P("gx", "gy", None, None),
        P("gx", "gy", None, None),
        P("gx", "gy", None, None),
    )
    out_specs = (P("gx", "gy", None, None, None), P("gy", "gx"))
    return jax.shard_map(
        functools.partial(per_device, grid), mesh=mesh, in_specs=in_specs, out_specs=out_specs, check_vma=False
    )


def solution(mesh):
    return build(mesh, 2, 2)
```

time: 77.6 us -> 62.3 us (0.80)
  the two profiles are of different devices: /device:TPU:1 before, /device:TPU:15 now
where the time goes in v2:
time: 62.3 us; the launch traced here: 62.2 us
  Pallas kernels  59.2 us (95%)
  local copies, waits for them, and re-layouts  2.37 us (4%)
  between operations  0.65 us (1%)
    pallas_call x1, Pallas kernels, per_device(): pl.pallas_call(functools.partial(kernel, gd), out_shape=(jax.ShapeDtypeSt...  59.2 us
    unnamed x4, local copies, waits for them, and re-layouts  2.37 us

profile of v2, /device:TPU:15, one launch (start us, length us, event | category | flops | bytes accessed | tf_op | source)
XLA Modules:
  0.0 62.2 jit_solution(12042275393486522135)
XLA Ops:
  0.6 59.2 %shard_map.95 = (bf16[12,128,128]{2,1,0:T(8,128)(2,1)}, f32[8,216]{1,0:T(8,128)}) custom-call(s32[7,1,27]{2,1,0:T(1,128)} %bitcast.19, s32[7,1,27]{2,1,0:T(1,128)} %bitcast.20, s32[2,8]{1,0:T(2,128)} %bitcast.21, bf16[12,128,128]{2,1,0:T(8,128)(2,1)} %bitcast.16, bf16[12,128,128]{2,1,0:T(8,128)(2,1)} %bitcast.17, bf16[12,128,128]{2,1,0:T(8,128)(2,1)} %bitcast.18, ...), custom_call_target="tpu_custom_call" | custom-call | flops 7927234560 | bytes 8388608 | tf_op jit(solution)/shard_map/pallas_call | solution.py:390
  59.8 0.0 copy-start
  59.8 1.8 %copy.12 = bf16[1,1,12,128,128]{4,3,2,1,0:T(8,128)(2,1)} copy(bf16[1,1,12,128,128]{4,3,2,1,0:T(8,128)(2,1)} %bitcast.14) | data formatting | bytes 786432
  61.6 0.0 copy-done
  61.6 0.6 copy.13
Async XLA Ops:
  59.8 1.8 %copy-start = (f32[8,216]{1,0:T(8,128)S(1)}, f32[8,216]{1,0:T(8,128)}, u32[]{:S(2)}) copy-start(f32[8,216]{1,0:T(8,128)} %get-tuple-element.5) | copy-start | bytes 20740

commit v3 on v2

--- a/solution.py
+++ b/solution.py
@@ -13,6 +13,7 @@
 HALO = 8 * SEND_CAP
 ZERO = BLOCKS + HALO
 SIDE = 14
+ORDER = (5, 7, 0, 2, 3, 4, 6, 1)
 MESH = pl.DeviceIdType.MESH
 F32, BF16 = jnp.float32, jnp.bfloat16
 
@@ -144,13 +145,25 @@
         for copy in copies:
             copy.wait_recv()
 
+    def inside(a, b):
+        px, qy = p + a, q + b
+        return (px >= 0) & (px < gd.n_gx) & (qy >= 0) & (qy < gd.n_gy)
+
+    def each_inside(copies, sign, act):
+        for e in ORDER:
+            a, b = HEADINGS[e]
+
+            @pl.when(inside(sign * a, sign * b))
+            def _():
+                act(copies[e])
+
+    def start_halo(copies, sign):
+        each_inside(copies, sign, lambda copy: copy.start())
+
     def arrive_halo(copies, buffer, first, sign):
-        arrive(copies)
+        each_inside(copies, -sign, lambda copy: copy.wait_recv())
         for e, (a, b) in enumerate(HEADINGS):
-            px, qy = p + sign * a, q + sign * b
-            inside = (px >= 0) & (px < gd.n_gx) & (qy >= 0) & (qy < gd.n_gy)
-
-            @pl.when(jnp.logical_not(inside))
+            @pl.when(jnp.logical_not(inside(-sign * a, -sign * b)))
             def _():
                 for s in range(SEND_CAP):
                     buffer[first + 2 * e + s] = zero_block
@@ -172,12 +185,12 @@
 
         lax.fori_loop(0, HALO // 4, group, 0)
 
-    def own_partial(grads, weight):
+    def own_partial(grads, weight, groups=(0, BLOCKS // 4)):
         def group(i, _):
             acc[pl.ds(4 * i, 4)] = products(grads, weight, 4 * i, 4)
             return 0
 
-        lax.fori_loop(0, BLOCKS // 4, group, 0)
+        lax.fori_loop(*groups, group, 0)
 
     def with_returned(b, layer):
         total = acc[b]
@@ -299,21 +312,22 @@
                     f_recv[places[x]] = f_send[layer, x * gd.quarter + i]
 
     pl.semaphore_wait(barrier, greeted)
-    start(act_copies)
+    start_halo(act_copies, 1)
     got_cot.wait()
     got_w2.wait()
     got_inv.wait()
     halo_partial(g_ext, w2, 1)
-    start(back_copies[1])
-    start(feat_copies)
+    start_halo(back_copies[1], -1)
     turn(g_ext)
-    own_partial(g_ext, w2)
+    own_partial(g_ext, w2, (0, 1))
+    start_halo(feat_copies, 1)
+    own_partial(g_ext, w2, (1, BLOCKS // 4))
     got_in_tab.wait()
     got_out_tab.wait()
-    arrive_halo(act_copies, act_ext, BLOCKS, -1)
+    arrive_halo(act_copies, act_ext, BLOCKS, 1)
     weight_terms(act_ext, 1)
     to_rings(1)
-    arrive_halo(back_copies[1], rb_g2, 0, 1)
+    arrive_halo(back_copies[1], rb_g2, 0, -1)
 
     def slope(b, _):
         value = pre[b].astype(F32)
@@ -325,21 +339,22 @@
     turn(pg_ext)
     got_feat_ext.wait()
     got_w1.wait()
-    arrive_halo(feat_copies, feat_ext, BLOCKS, -1)
+    arrive_halo(feat_copies, feat_ext, BLOCKS, 1)
     weight_terms(feat_ext, 0)
     to_rings(0)
     halo_partial(pg_ext, w1, 0)
-    start(back_copies[0])
+    start_halo(back_copies[0], -1)
     to_holders(1)
     own_partial(pg_ext, w1)
     to_holders(0)
-    arrive_halo(back_copies[0], rb_g1, 0, 1)
+    arrive_halo(back_copies[0], rb_g1, 0, -1)
 
     def finish(b, _):
-        grad_out[b] = with_returned(b, 0).astype(BF16)
+        grad_out[b] = with_returned(b, 0)
         return 0
 
     lax.fori_loop(0, BLOCKS, finish, 0)
+
     stored = load(12, grad_out, grad_hbm)
 
     own_place = jnp.where(xl == 0, places[0], places[1])
@@ -357,11 +372,12 @@
     total = f_recv[0].astype(F32)
     for s in range(1, gd.sources):
         total = total + f_recv[s].astype(F32)
-    total = total * (1.0 / math.sqrt(MAP_CAP * BLOCK * gd.n_gx * gd.n_gy))
     total = jnp.concatenate([total[:gd.columns], total[gd.columns:]], axis=1)
     weight_out[...] = total[:, :gd.rows]
 
-    for copies in [act_copies, feat_copies, core_copies] + back_copies + ring_copies[0] + ring_copies[1]:
+    for copies, sign in ((act_copies, 1), (feat_copies, 1), (back_copies[0], -1), (back_copies[1], -1)):
+        each_inside(copies, sign, lambda copy: copy.wait_send())
+    for copies in [core_copies] + ring_copies[0] + ring_copies[1]:
         for copy in copies:
             copy.wait_send()
     for layer in range(2):
@@ -385,16 +401,16 @@
     dma = pltpu.SemaphoreType.DMA
     block = (BLOCK, 128)
     slots = (MAP_CAP, 1, KERNEL)
-    hbm = pl.BlockSpec(memory_space=pltpu.HBM)
+    hbm, vmem = pl.BlockSpec(memory_space=pltpu.HBM), pl.BlockSpec(memory_space=pltpu.VMEM)
     flops = 2 * 128 ** 3 * KERNEL * 2 * (ZERO + MAP_CAP)
     grad, weight = pl.pallas_call(
         functools.partial(kernel, gd),
         out_shape=(
-            jax.ShapeDtypeStruct((BLOCKS,) + block, BF16),
+            jax.ShapeDtypeStruct((BLOCKS,) + block, F32),
             jax.ShapeDtypeStruct((gd.columns, gd.rows), F32),
         ),
         in_specs=[hbm] * 8,
-        out_specs=(hbm, pl.BlockSpec(memory_space=pltpu.VMEM)),
+        out_specs=(hbm, vmem),
         scratch_shapes=[
             pltpu.VMEM(slots, jnp.int32),
             pltpu.VMEM(slots, jnp.int32),
@@ -407,7 +423,7 @@
             pltpu.VMEM((BLOCKS,) + block, BF16),
             pltpu.VMEM((KERNEL,) + block, BF16),
             pltpu.VMEM((KERNEL,) + block, BF16),
-            pltpu.VMEM((BLOCKS,) + block, BF16),
+            pltpu.VMEM((BLOCKS,) + block, F32),
             pltpu.VMEM((BLOCKS,) + block, BF16),
             pltpu.VMEM((ext,) + block, BF16),
             pltpu.VMEM((ext,) + block, BF16),
@@ -443,7 +459,8 @@
         ),
         cost_estimate=pl.CostEstimate(flops=flops, bytes_accessed=8 * 2 ** 20, transcendentals=0),
     )(slots_in, slots_out, sends, features_in[0, 0], pre_act[0, 0], cotangent[0, 0], w_first, w_second)
-    return grad[None, None], weight.T
+    weight = weight.T * (1.0 / math.sqrt(MAP_CAP * BLOCK * gd.n_gx * gd.n_gy))
+    return grad.astype(BF16)[None, None], weight
 
 
 def build(mesh, x_lo, x_hi):

time: 62.3 us -> 60.7 us (0.974)
  the two profiles are of different devices: /device:TPU:15 before, /device:TPU:1 now
where the time goes in v3:
time: 60.7 us; the launch traced here: 60.1 us
  Pallas kernels  56.9 us (94%)
  other arithmetic  2.55 us (4%)
  between operations  0.65 us (1%)
    pallas_call x1, Pallas kernels, per_device(): pl.pallas_call(functools.partial(kernel, gd), out_shape=(jax.ShapeDtypeSt...  56.9 us
    broadcast_in_dim x1, other arithmetic, per_device(): return (grad.astype(BF16)[None, None], weight)  1.95 us

profile of v3, /device:TPU:1, one launch (start us, length us, event | category | flops | bytes accessed | tf_op | source)
XLA Modules:
  0.0 60.1 jit_solution(8623122086806318052)
XLA Ops:
  0.6 56.9 %shard_map.95 = (f32[12,128,128]{2,1,0:T(8,128)}, f32[8,216]{1,0:T(8,128)}) custom-call(s32[7,1,27]{2,1,0:T(1,128)} %bitcast.19, s32[7,1,27]{2,1,0:T(1,128)} %bitcast.20, s32[2,8]{1,0:T(2,128)} %bitcast.21, bf16[12,128,128]{2,1,0:T(8,128)(2,1)} %bitcast.16, bf16[12,128,128]{2,1,0:T(8,128)(2,1)} %bitcast.17, bf16[12,128,128]{2,1,0:T(8,128)(2,1)} %bitcast.18, ...), custom_call_target="tpu_custom_call" | custom-call | flops 7927234560 | bytes 8388608 | tf_op jit(solution)/shard_map/pallas_call | solution.py:406
  57.5 0.0 copy-start
  57.5 2.0 %convert_bitcast_fusion = bf16[1,1,12,128,128]{4,3,2,1,0:T(8,128)(2,1)} fusion(f32[12,128,128]{2,1,0:T(8,128)} %get-tuple-element.4), kind=kLoop, calls=%fused_computation | loop fusion | flops 196608 | bytes 1179648 | tf_op jit(solution)/shard_map/broadcast_in_dim | solution.py:463
  59.5 0.0 copy-done
  59.5 0.6 multiply_bitcast_fusion
Async XLA Ops:
  57.5 2.0 %copy-start = (f32[8,216]{1,0:T(8,128)S(1)}, f32[8,216]{1,0:T(8,128)}, u32[]{:S(2)}) copy-start(f32[8,216]{1,0:T(8,128)} %get-tuple-element.5) | copy-start | bytes 20740

commit v4 on v3

--- a/solution.py
+++ b/solution.py
@@ -151,6 +151,7 @@
 
     def each_inside(copies, sign, act):
         for e in ORDER:
+            e = e if sign > 0 else 7 - e
             a, b = HEADINGS[e]
 
             @pl.when(inside(sign * a, sign * b))

time: 60.7 us -> 60.7 us (level)
  no operation moved by 1% of the time
where the time goes in v4:
time: 60.7 us; the launch traced here: 60 us
  Pallas kernels  56.7 us (93%)
  other arithmetic  2.55 us (4%)
  between operations  0.65 us (1%)
    pallas_call x1, Pallas kernels, per_device(): pl.pallas_call(functools.partial(kernel, gd), out_shape=(jax.ShapeDtypeSt...  56.7 us
    broadcast_in_dim x1, other arithmetic, per_device(): return (grad.astype(BF16)[None, None], weight)  1.95 us

profile of v4, /device:TPU:1, one launch (start us, length us, event | category | flops | bytes accessed | tf_op | source)
XLA Modules:
  0.0 60.0 jit_solution(15457331891645685778)
XLA Ops:
  0.6 56.7 %shard_map.95 = (f32[12,128,128]{2,1,0:T(8,128)}, f32[8,216]{1,0:T(8,128)}) custom-call(s32[7,1,27]{2,1,0:T(1,128)} %bitcast.19, s32[7,1,27]{2,1,0:T(1,128)} %bitcast.20, s32[2,8]{1,0:T(2,128)} %bitcast.21, bf16[12,128,128]{2,1,0:T(8,128)(2,1)} %bitcast.16, bf16[12,128,128]{2,1,0:T(8,128)(2,1)} %bitcast.17, bf16[12,128,128]{2,1,0:T(8,128)(2,1)} %bitcast.18, ...), custom_call_target="tpu_custom_call" | custom-call | flops 7927234560 | bytes 8388608 | tf_op jit(solution)/shard_map/pallas_call | solution.py:407
  57.4 0.0 copy-start
  57.4 2.0 %convert_bitcast_fusion = bf16[1,1,12,128,128]{4,3,2,1,0:T(8,128)(2,1)} fusion(f32[12,128,128]{2,1,0:T(8,128)} %get-tuple-element.4), kind=kLoop, calls=%fused_computation | loop fusion | flops 196608 | bytes 1179648 | tf_op jit(solution)/shard_map/broadcast_in_dim | solution.py:464
  59.3 0.0 copy-done
  59.4 0.6 %multiply_bitcast_fusion = f32[216,8]{0,1:T(8,128)} fusion(f32[8,216]{1,0:T(8,128)S(1)} %copy-done), kind=kLoop, calls=%fused_computation.1 | loop fusion | flops 1728 | bytes 13824 | tf_op jit(solution)/shard_map/mul | solution.py:463
Async XLA Ops:
  57.4 2.0 %copy-start = (f32[8,216]{1,0:T(8,128)S(1)}, f32[8,216]{1,0:T(8,128)}, u32[]{:S(2)}) copy-start(f32[8,216]{1,0:T(8,128)} %get-tuple-element.5) | copy-start | bytes 20740
